TPU v7x, 32 devices: a whole 2x2x4 slice. The times are simulated.
32 devices in a mesh: group: 1, ctx: 16 (over z, y, x), head: 2 (over core).
Axes of the slice: x: 2, y: 2, z: 4, core: 2. Of those that a mesh axis runs over, the one named last changes fastest.
Arguments:
- pair_raw: bfloat16 [4096, 2, 1024], P(('group', 'ctx'), None, 'head'), may hold values from -6 to 6
- value_raw: bfloat16 [4096, 2048], P(('group', 'ctx'), 'head'), may hold values from -6 to 6
- gate_raw: bfloat16 [4096, 2048], P(('group', 'ctx'), 'head'), may hold values from -6 to 6
- write_strength: float32 [4096, 16], P(('group', 'ctx'), 'head'), may hold values from 0.05 to 0.95
- log_decay: float32 [4096, 16], P(('group', 'ctx'), 'head'), may hold values from -2.6 to 0
- segment_ids: int32 [4096], P('group'), may hold values from 0 to 1, never falling along the last dimension, each value on 1 to 3968 neighbouring positions
- pair_filter: float32 [4, 2, 1024], P(None, None, 'head'), may hold values from -3 to 3
- value_filter: float32 [4, 2048], P(None, 'head'), may hold values from -3 to 3
- norm_gain: float32 [128], replicated, may hold values from 0.1 to 1.9
- out_weight: bfloat16 [2048, 2048], P('head'), may hold values from -0.125 to 0.125
- residual: bfloat16 [4096, 2048], P(('group', 'ctx', 'head')), may hold values from -27 to 27
- post_gain: float32 [2048], replicated, may hold values from 0.1 to 1.9
- routes: int32 [4096, 10], P(('group', 'ctx', 'head')), may hold values from 0 to 31, all different within a row; in each aligned block of 128 rows (0 to 127, 128 to 255, ...) at most 50 rows name the same one
- route_weights: float32 [4096, 10], P(('group', 'ctx', 'head')), may hold values from 0.05 to 0.3
- expert_up: bfloat16 [32, 2048, 1024], P(('ctx', 'head')), may hold values from -0.125 to 0.125
- expert_down: bfloat16 [32, 512, 2048], P(('ctx', 'head')), may hold values from -0.25 to 0.25
Outputs:
- layer_out: bfloat16 [4096, 2048], P(('group', 'ctx', 'head'))
Inputs may be any that keep to these rules, and one draw needn't show every extreme that they name: `routes`: in each aligned block of 128 rows (the rows of one device) no expert is named by more than 50 rows; a row names 10 different experts. `segment_ids`: rollout numbers never fall along the slab; a rollout holds 1 to 3968 tokens of the slab.
All inputs are finite; a program needn't handle non-finite values.
Results may differ from a plain program's by a relative error of at most 0.012.
Values may be sent and summed in bfloat16 or wider, within the bound.
A program may use at most 128 MiB of HBM per device.

v0:
```python
import jax
import jax.numpy as jnp
from jax import lax
from jax.sharding import PartitionSpec as P

D = 2048
DK = 128
DV = 128
BLOCK = 64


HIGHEST = lax.Precision.HIGHEST


def passed_along(block, axis, distance):
    devices = range(lax.axis_size(axis))
    route = [(i - distance, i) for i in devices if i - distance in devices]
    return lax.ppermute(block, axis, route)


def carried_in_2(shard, axis, combine, identity):
    peers, position = (lax.axis_size(axis), lax.axis_index(axis))
    everything = jax.tree.map(
        lambda part, kind: lax.all_gather(part.astype(kind), axis),
        shard,
        (jnp.bfloat16, jnp.bfloat16),
    )
    start = jax.tree.map(
        lambda part, zero: jnp.broadcast_to(jnp.asarray(zero, part.dtype), part.shape),
        shard,
        identity,
    )

    def step(k, before):
        reached = k < position
        new = combine(
            before, jax.tree.map(lambda part, own: part[k].astype(own.dtype), everything, shard)
        )
        return jax.tree.map(lambda a, b: jnp.where(reached, a, b), new, before)

    return lax.fori_loop(0, peers, step, start)


def precise_dot(left, right):
    return jnp.dot(left, right, precision=HIGHEST, preferred_element_type=jnp.float32)


def causal_filter(padded_raw, filter_taps, padded_ids, kernel):
    length = padded_raw.shape[0] - (kernel - 1)
    source = padded_raw.astype(jnp.float32)
    current_ids = padded_ids[kernel - 1 :]
    summed = jnp.zeros((length, padded_raw.shape[1]), jnp.float32)
    for lag_step in range(kernel):
        offset_start = kernel - 1 - lag_step
        shifted = source[offset_start : offset_start + length]
        matching = (padded_ids[offset_start : offset_start + length] == current_ids).astype(
            jnp.float32
        )
        summed = summed + filter_taps[lag_step] * shifted * matching[:, None]
    return jax.nn.silu(summed)


def unit_rows(values_in):
    return values_in / jnp.sqrt(jnp.sum(values_in * values_in, axis=-1, keepdims=True) + 1e-06)


def mixer_inputs(pair_padded, value_padded, pair_filter, value_filter, padded_ids, kernel):
    pair_act = causal_filter(pair_padded, pair_filter.reshape(kernel, -1), padded_ids, kernel)
    length = pair_act.shape[0]
    pair_heads = pair_act.reshape(length, 2, -1, DK)
    queries = unit_rows(pair_heads[:, 0]) * DK ** (-0.5)
    key_rows = unit_rows(pair_heads[:, 1])
    value_rows = causal_filter(value_padded, value_filter, padded_ids, kernel).reshape(
        length, -1, DV
    )
    repeat_factor = value_rows.shape[1] // key_rows.shape[1]
    return (
        jnp.repeat(queries, repeat_factor, axis=1),
        jnp.repeat(key_rows, repeat_factor, axis=1),
        value_rows,
    )


def block_setup(queries, key_rows, value_rows, strength, decay_rows, segment_here, prior_id):
    cumulative = jnp.cumsum(decay_rows)
    row_index = lax.broadcasted_iota(jnp.int32, (BLOCK, BLOCK), 0)
    col_index = lax.broadcasted_iota(jnp.int32, (BLOCK, BLOCK), 1)
    same_segment = segment_here[:, None] == segment_here[None, :]
    causal = (row_index >= col_index) & same_segment
    strictly = (row_index > col_index) & same_segment
    decay_matrix = jnp.where(
        causal, jnp.exp(jnp.where(causal, cumulative[:, None] - cumulative[None, :], 0.0)), 0.0
    )
    carried_in = (segment_here == prior_id).astype(jnp.float32)
    keyed_beta = key_rows * strength[:, None]
    coupling = jnp.where(strictly, precise_dot(keyed_beta, key_rows.T) * decay_matrix, 0.0)
    system = jnp.eye(BLOCK, dtype=jnp.float32) + coupling
    stacked = jnp.concatenate(
        [value_rows * strength[:, None], keyed_beta * (jnp.exp(cumulative) * carried_in)[:, None]],
        axis=1,
    )
    solved = lax.linalg.triangular_solve(
        system, stacked, left_side=True, lower=True, unit_diagonal=True
    )
    targets = solved[:, :DV]
    corrector = solved[:, DV:]
    within = jnp.where(causal, precise_dot(queries, key_rows.T) * decay_matrix, 0.0)
    query_decayed = queries * (jnp.exp(cumulative) * carried_in)[:, None]
    final_log = cumulative[BLOCK - 1]
    weighting = (segment_here == segment_here[BLOCK - 1]).astype(jnp.float32) * jnp.exp(
        final_log - cumulative
    )
    keys_weighted = key_rows * weighting[:, None]
    transition = jnp.exp(final_log) * carried_in[BLOCK - 1] * jnp.eye(
        DK, dtype=jnp.float32
    ) - precise_dot(keys_weighted.T, corrector)
    increment = precise_dot(keys_weighted.T, targets)
    return (within, query_decayed, targets, corrector, transition, increment)


def head_major(array_in, block_count):
    moved = jnp.moveaxis(array_in, 1, 0)
    return moved.reshape((array_in.shape[1], block_count, BLOCK) + array_in.shape[2:])


def block_tables(queries, key_rows, value_rows, strength, decay_rows, padded_ids, kernel):
    length = queries.shape[0]
    block_count = length // BLOCK
    current_ids = padded_ids[kernel - 1 :].reshape(block_count, BLOCK)
    prior_ids = padded_ids[kernel - 2 : kernel - 2 + length : BLOCK]
    per_block = jax.vmap(block_setup, in_axes=(0, 0, 0, 0, 0, 0, 0))
    per_head = jax.vmap(per_block, in_axes=(0, 0, 0, 0, 0, None, None))
    return per_head(
        head_major(queries, block_count),
        head_major(key_rows, block_count),
        head_major(value_rows, block_count),
        head_major(strength, block_count),
        head_major(decay_rows, block_count),
        current_ids,
        prior_ids,
    )


def batched(left, right):
    return jnp.einsum("hij,hjk->hik", left, right, precision=HIGHEST)


def sweep_blocks(block_terms, start_state):
    blocks_first = tuple((jnp.swapaxes(member, 0, 1) for member in block_terms))

    def advance(carry_state, pieces):
        within, query_decayed, targets, corrector, transition, increment = pieces
        fresh_values = targets - batched(corrector, carry_state)
        emitted = batched(query_decayed, carry_state) + batched(within, fresh_values)
        updated = batched(transition, carry_state) + increment
        return (updated, emitted)

    final_state, emitted = lax.scan(advance, start_state, blocks_first)
    return emitted


def tokens_first(emitted):
    heads_count = emitted.shape[1]
    return jnp.transpose(emitted, (0, 2, 1, 3)).reshape(-1, heads_count, emitted.shape[3])


def gate_output(mixed_heads, gate_raw, norm_gain):
    square_mean = jnp.mean(mixed_heads * mixed_heads, axis=-1, keepdims=True)
    gate_values = jax.nn.silu(gate_raw.reshape(mixed_heads.shape).astype(jnp.float32))
    normed = mixed_heads / jnp.sqrt(square_mean + 1e-06) * norm_gain * gate_values
    return normed.astype(jnp.bfloat16).reshape(mixed_heads.shape[0], -1)


def post_norm(hidden, post_gain):
    hidden_full = hidden.astype(jnp.float32)
    square_mean = jnp.mean(hidden_full * hidden_full, axis=-1, keepdims=True)
    return (hidden_full / jnp.sqrt(square_mean + 1e-06) * post_gain).astype(jnp.bfloat16)


def expert_apply_rows(rows_in, up_matrix, down_matrix):
    hidden_units = down_matrix.shape[0]
    gate_up = jnp.dot(rows_in, up_matrix, preferred_element_type=jnp.float32)
    activated = (jax.nn.silu(gate_up[:, :hidden_units]) * gate_up[:, hidden_units:]).astype(
        jnp.bfloat16
    )
    return jnp.dot(activated, down_matrix, preferred_element_type=jnp.float32).astype(jnp.bfloat16)


def expert_apply(arrived, expert_up, expert_down):
    member_rows = arrived[:, 0]
    flattened = member_rows.reshape(-1, member_rows.shape[-1])
    result = expert_apply_rows(flattened, expert_up[0], expert_down[0])
    outputs = [result.reshape(member_rows.shape)]
    return jnp.stack(outputs, axis=1)


def route_slots(routes, experts_all, capacity):
    assigned = routes.reshape(-1)
    expert_ids = jnp.arange(experts_all, dtype=jnp.int32)
    onehot = (assigned[:, None] == expert_ids[None, :]).astype(jnp.int32)
    slot_rank = jnp.sum((jnp.cumsum(onehot, axis=0) - 1) * onehot, axis=1)
    return assigned * capacity + slot_rank


def per_device(
    pair_raw,
    value_raw,
    gate_raw,
    write_strength,
    log_decay,
    segment_ids,
    pair_filter,
    value_filter,
    norm_gain,
    out_weight,
    residual,
    post_gain,
    routes,
    route_weights,
    expert_up,
    expert_down,
):
    local_tokens = pair_raw.shape[0]
    kernel = value_filter.shape[0]
    pair_flat = pair_raw.reshape(local_tokens, -1)
    pair_width = pair_flat.shape[1]
    rim_rows = jnp.concatenate(
        [pair_flat[local_tokens - (kernel - 1) :], value_raw[local_tokens - (kernel - 1) :]], axis=1
    )
    before = passed_along(rim_rows, "ctx", 1)
    first_token = lax.axis_index("ctx") * local_tokens
    padded_ids = jnp.concatenate([jnp.full((kernel - 1,), -1, jnp.int32), segment_ids])
    window_ids = lax.dynamic_slice_in_dim(padded_ids, first_token, local_tokens + kernel - 1)
    pair_padded = jnp.concatenate([before[:, :pair_width], pair_flat])
    value_padded = jnp.concatenate([before[:, pair_width:], value_raw])
    queries, key_rows, value_rows = mixer_inputs(
        pair_padded, value_padded, pair_filter, value_filter, window_ids, kernel
    )
    block_terms = block_tables(
        queries, key_rows, value_rows, write_strength, log_decay, window_ids, kernel
    )
    heads_here = value_rows.shape[1]
    identity_maps = jnp.broadcast_to(jnp.eye(DK, dtype=jnp.float32), (heads_here, DK, DK))
    empty_state = jnp.zeros((heads_here, DK, DV), jnp.float32)

    def fold_block(totals, pieces):
        transition, increment = pieces
        return ((batched(transition, totals[0]), batched(transition, totals[1]) + increment), None)

    whole_pair, unused = lax.scan(
        fold_block,
        (identity_maps, empty_state),
        (jnp.swapaxes(block_terms[4], 0, 1), jnp.swapaxes(block_terms[5], 0, 1)),
    )
    whole_map, whole_shift = whole_pair

    def join_pairs(earlier, later):
        return (batched(later[0], earlier[0]), batched(later[0], earlier[1]) + later[1])

    prefix = carried_in_2((whole_map, whole_shift), "ctx", join_pairs, (identity_maps, empty_state))
    entering = prefix[1]
    emitted = sweep_blocks(block_terms, entering)
    gated_out = gate_output(tokens_first(emitted), gate_raw, norm_gain)
    attention = lax.psum_scatter(
        jnp.dot(gated_out, out_weight, preferred_element_type=jnp.float32).astype(jnp.bfloat16),
        "head",
        scatter_dimension=0,
        tiled=True,
    ).astype(jnp.float32)
    hidden = (residual.astype(jnp.float32) + attention).astype(jnp.bfloat16)
    expert_in = post_norm(hidden, post_gain)
    devices_all = lax.axis_size("ctx") * lax.axis_size("head")
    local_experts = expert_up.shape[0]
    experts_all = devices_all * local_experts
    local_rows = routes.shape[0]
    top_count = routes.shape[1]
    capacity = local_rows * top_count * 5 // (4 * experts_all)
    slot_index = route_slots(routes, experts_all, capacity)
    owners = jnp.arange(local_rows * top_count, dtype=jnp.int32) // top_count + 1
    owner_table = jnp.zeros((experts_all * capacity,), jnp.int32).at[slot_index].set(owners)
    filled = owner_table > 0
    outgoing = jnp.where(
        filled[:, None], expert_in[jnp.maximum(owner_table - 1, 0)], jnp.zeros((), jnp.bfloat16)
    )
    outgoing = outgoing.reshape(devices_all, local_experts, capacity, D)
    answered = expert_apply(
        lax.all_to_all(outgoing, ("ctx", "head"), split_axis=0, concat_axis=0, tiled=True),
        expert_up,
        expert_down,
    )
    returned = lax.all_to_all(answered, ("ctx", "head"), split_axis=0, concat_axis=0, tiled=True)
    result_rows = returned.reshape(-1, D)
    chosen_slots = slot_index.reshape(local_rows, top_count)
    combined = hidden.astype(jnp.float32)
    for column in range(top_count):
        combined = combined + route_weights[:, column : column + 1] * result_rows[
            chosen_slots[:, column]
        ].astype(jnp.float32)
    return combined.astype(jnp.bfloat16)


def solution(mesh):
    return jax.shard_map(
        per_device,
        mesh=mesh,
        in_specs=(
            P(("group", "ctx"), None, "head"),
            P(("group", "ctx"), "head"),
            P(("group", "ctx"), "head"),
            P(("group", "ctx"), "head"),
            P(("group", "ctx"), "head"),
            P("group"),
            P(None, None, "head"),
            P(None, "head"),
            P(),
            P("head", None),
            P(("group", "ctx", "head"), None),
            P(),
            P(("group", "ctx", "head"), None),
            P(("group", "ctx", "head"), None),
            P(("ctx", "head"), None, None),
            P(("ctx", "head"), None, None),
        ),
        out_specs=P(("group", "ctx", "head"), None),
        check_vma=False,
    )
```

profile of v0, /device:TPU:0, one launch (start us, length us, event | category | flops | bytes accessed | tf_op | source)
XLA Modules:
  0.0 924.0 jit_solution(10823575093657929736)
XLA Ops:
  8.1 4.8 collective-permute-start
  21.9 2.9 multiply_bitcast_fusion.1
  24.7 1.7 reshape.270
  29.9 3.1 fusion.63
  33.0 158.7 %custom-call.3 = f32[8,4,1,64,64]{3,4,2,1,0:T(8,128)} custom-call(f32[8,4,1,64,64]{4,3,2,1,0:T(8,128)} %fusion.63), custom_call_target="InvertDiagBlocksLowerTriangular" | custom-call | tf_op jit(solution)/shard_map/vmap(vmap())/triangular_solve | solution.py:102
  192.8 3.1 multiply_bitcast_fusion
  196.0 2.0 fusion.37
  198.0 3.8 convolution_bitcast_fusion
  203.2 4.0 bitcast_subtract_fusion
  208.8 14.7 %while.40 = (s32[]{:T(128)}, f32[8,128,128]{2,1,0:T(8,128)S(1)}, f32[8,128,128]{2,1,0:T(8,128)S(1)}, f32[4,8,128,128]{3,2,1,0:T(8,128)}, f32[4,8,128,128]{3,2,1,0:T(8,128)}, /*index=5*/s32[]{:T(128)}, s32[]{:T(128)}) while((s32[]{:T(128)}, f32[8,128,128]{2,1,0:T(8,128)S(1)}, f32[8,128,128]{2,1,0:T(8,128)S(1)}, ...), condition=%wide.region_3.4_spmd.clone, body=%wide.region_2.3_spmd.clone.sunk | while | flops 402915328 | bytes 5768791 | solution.py:250
  208.9 1.8 convolution_add_fusion.7
  210.8 1.7 fusion.180
  212.6 1.8 convolution_add_fusion.7
  214.5 1.7 fusion.180
  216.3 1.8 convolution_add_fusion.7
  218.2 1.7 fusion.180
  219.9 1.8 convolution_add_fusion.7
  221.8 1.7 fusion.180
  225.7 3.2 slice_bitcast_fusion.1
  228.9 2.9 fusion.50
  231.8 69.1 %all-gather.5.cloned.1.call-done = bf16[128,128,128]{2,1,0:T(8,128)(2,1)} async-done(((bf16[8,128,128]{2,1,0:T(8,128)(2,1)}), bf16[128,128,128]{2,1,0:T(8,128)(2,1)}) %all-gather.5.cloned.1.call-update) | async-done | bytes 4194320 | tf_op jit(solution)/shard_map/all_gather | solution.py:24
  300.9 77.5 %all-gather.7.cloned.1.call-done = bf16[128,128,128]{2,1,0:T(8,128)(2,1)} async-done(((bf16[8,128,128]{2,1,0:T(8,128)(2,1)}), bf16[128,128,128]{2,1,0:T(8,128)(2,1)}) %all-gather.7.cloned.1.call-update) | async-done | bytes 4194320 | tf_op jit(solution)/shard_map/all_gather | solution.py:24
  378.4 25.3 %while.41 = (s32[]{:T(128)}, f32[8,128,128]{2,1,0:T(8,128)S(1)}, s32[]{:T(128)}, bf16[16,8,128,128]{3,2,1,0:T(8,128)(2,1)}, bf16[16,8,128,128]{3,2,1,0:T(8,128)(2,1)}, /*index=5*/s32[]{:T(128)}, s32[]{:T(128)}) while((s32[]{:T(128)}, f32[8,128,128]{2,1,0:T(8,128)S(1)}, s32[]{:T(128)}, bf16[16,8,128,128]{3,2,1,0:T(8,128)(2,1)}, ...), condition=%wide.region_5.6_spmd.clone, body=%wide.region_4.5_spmd.clone.sunk | while | flops 201981952 | bytes 3148383 | solution.py:41
  403.7 28.7 %while.39 = (s32[]{:T(128)}, f32[8,128,128]{2,1,0:T(8,128)S(1)}, f32[4,8,64,128]{3,2,1,0:T(8,128)}, f32[4,8,128,128]{3,2,1,0:T(8,128)}, f32[4,8,128,128]{3,2,1,0...) while((s32[]{:T(128)}, f32[8,128,128]{2,1,0:T(8,128)S(1)}, ...), condition=%wide.region_8.9_spmd, body=%wide.region_7.8_spmd.sunk | while | flops 453246976 | bytes 6557285 | solution.py:158
  403.7 1.6 convolution_subtract_fusion.2
  406.9 2.1 fusion.175
  409.0 1.8 convolution_add_fusion.6
  410.9 1.6 convolution_subtract_fusion.2
  414.1 2.1 fusion.175
  416.2 1.8 convolution_add_fusion.6
  418.1 1.6 convolution_subtract_fusion.2
  419.7 1.6 fusion.174
  421.3 2.1 fusion.175
  423.3 1.8 convolution_add_fusion.6
  425.2 1.6 convolution_subtract_fusion.2
  428.4 2.1 fusion.175
  430.5 1.8 convolution_add_fusion.6
  432.4 1.6 multiply_reduce_fusion
  434.1 1.8 copy.141
  436.3 4.7 convolution_convert_fusion.1
  441.4 9.1 reduce-window.6
  451.5 5.2 scatter_custom_fusion
  459.6 7.7 gather_fusion
  467.3 8.7 gather.36
  475.9 3.7 select_bitcast_fusion
  479.6 164.2 %all_to_all.10 = bf16[32,1,50,2048]{3,2,1,0:T(8,128)(2,1)} all-to-all(bf16[32,1,50,2048]{3,2,1,0:T(8,128)(2,1)S(1)} %select_bitcast_fusion), channel_id=1, replica_groups=mesh['group'=1,'ctx'=16,'head'=2] {'ctx','head'}, dimensions={0} | all-to-all | bytes 13107200 | tf_op jit(solution)/shard_map/all_to_all | solution.py:287
  643.8 8.8 reshape_squeeze.3
  652.6 10.3 %fusion.34 = f32[1600,1024]{1,0:T(8,128)S(1)} fusion(bf16[1600,2048]{1,0:T(8,128)(2,1)} %reshape_squeeze.3, bf16[1,2048,1024]{2,1,0:T(8,128)(2,1)} %param.36), kind=kOutput, calls=%fused_computation.53 | convolution fusion | flops 6710886400 | bytes 17301504 | tf_op jit(solution)/shard_map/dot_general | solution.py:182
  662.9 5.5 convolution_convert_fusion
  668.4 8.7 stack_reshape.3
  677.1 3.9 all-to-all-start.1
  681.5 162.6 %all-to-all-done.1 = bf16[32,1,50,2048]{3,2,1,0:T(8,128)(2,1)} async-done(((bf16[32,1,50,2048]{3,2,1,0:T(8,128)(2,1)}), bf16[32,1,50,2048]{3,2,1,0:T(8,128)(2,1)}, u32[]{:S(2)}, u32[]{:S(2)}) %all-to-all-start.1) | async-done | bytes 6553632 | tf_op jit(solution)/shard_map/all_to_all | solution.py:291
  844.1 8.9 reshape.279
  853.0 6.0 gather_fusion.1
  859.0 5.9 gather_fusion.2
  864.9 6.0 gather_fusion.3
  870.9 5.9 gather_fusion.4
  876.8 6.0 gather_fusion.5
  882.8 6.0 gather_fusion.6
  888.7 6.2 gather_fusion.7
  894.9 5.9 gather_fusion.8
  900.8 6.0 gather_fusion.9
  906.8 6.0 gather_fusion.10
  912.8 4.5 fusion.82
  (176 shorter events, 54.7 us)
Async XLA Ops:
  6.5 656.3 %copy-start = (bf16[1,512,2048]{2,1,0:T(8,128)(2,1)S(1)}, bf16[1,512,2048]{2,1,0:T(8,128)(2,1)}, u32[]{:S(2)}) copy-start(bf16[1,512,2048]{2,1,0:T(8,128)(2,1)} %param.37) | copy-start | bytes 6291460
  6.5 294.4 %all-gather.5.cloned.1.call-start = ((), (), s32[]{:S(2)}) async-start(), calls=%async_computation.4 | async-start | bytes 4456448 | tf_op jit(solution)/shard_map/all_gather | solution.py:24
  8.1 12.3 %collective-permute-start = (bf16[3,2048]{1,0:T(4,128)(2,1)S(1)}, bf16[3,2048]{1,0:T(4,128)(2,1)S(1)}, u32[]{:S(2)}, u32[]{:S(2)}) collective-permute-start(bf16[3,2048]{1,0:T(4,128)(2,1)S(1)} %pad_maximum_fusion), channel_id=1, source_target_pairs={{0,2},{2,4},{4,6},{6,8},{8,10},{10,12},{12,14},{14,16},{16,18},{18... | collective-permute-start | bytes 36872 | tf_op jit(solution)/shard_map/ppermute | solution.py:18
  26.4 2.4 copy-start.9
  29.9 173.3 %copy-start.1 = (f32[256,4,2,128]{3,0,2,1:T(8,128)}, f32[256,4,2,128]{3,0,2,1:T(8,128)S(1)}, u32[]{:S(2)}) copy-start(f32[256,4,2,128]{3,0,2,1:T(8,128)S(1)} %broadcast_in_dim.52) | copy-start | bytes 3145732
  192.8 3.1 copy-start.5
  192.8 3.1 copy-start.10
  198.0 5.3 copy-start.4
  207.2 1.6 copy-start.3
  208.8 16.8 %copy-start.14 = (f32[128]{0:T(128)S(1)}, f32[128]{0:T(128)}, u32[]{:S(2)}) copy-start(f32[128]{0:T(128)} %param.30) | copy-start | bytes 1540
  224.3 154.0 %all-gather.7.cloned.1.call-start = ((), (), s32[]{:S(2)}) async-start(), calls=%async_computation.5 | async-start | bytes 4456448 | tf_op jit(solution)/shard_map/all_gather | solution.py:24
  225.1 231.8 %reduce-scatter.2.cloned.1.call-start = ((), (), s32[]{:S(2)}) async-start(), calls=%async_computation.3 | async-start | bytes 1572864 | tf_op jit(solution)/shard_map/reduce_scatter | solution.py:264
  225.6 3.3 copy-start.2
  225.6 3.3 copy-start.6
  432.3 3.9 copy-start.15
  436.3 4.7 copy-start.12
  441.0 16.0 %copy-start.7 = (bf16[128,2048]{1,0:T(8,128)(2,1)S(1)}, bf16[128,2048]{1,0:T(8,128)(2,1)}, u32[]{:S(2)}) copy-start(bf16[128,2048]{1,0:T(8,128)(2,1)} %param.32) | copy-start | bytes 1572868
  441.0 17.3 %copy-start.11 = (f32[2048]{0:T(1024)S(1)}, f32[2048]{0:T(1024)}, u32[]{:S(2)}) copy-start(f32[2048]{0:T(1024)} %param.33) | copy-start | bytes 24580
  677.1 4.5 copy-start.13
  677.1 167.1 %all-to-all-start.1 = ((bf16[32,1,50,2048]{3,2,1,0:T(8,128)(2,1)}), bf16[32,1,50,2048]{3,2,1,0:T(8,128)(2,1)}, u32[]{:S(2)}, u32[]{:S(2)}) async-start(bf16[32,1,50,2048]{3,2,1,0:T(8,128)(2,1)} %bitcast.230), calls=%async_computation.2 | async-start | bytes 14680064 | tf_op jit(solution)/shard_map/all_to_all | solution.py:291
  906.8 6.0 copy-start.8
Sparse Core Ops, SparseCore 0:
  224.5 76.3 all-gather.4
  303.7 74.6 all-gather.6
  441.1 7.1 reduce-scatter.1
where the time goes:
time: 932 us; the launch traced here: 924 us
  waiting for transfers between devices  309 us (33%)
  other arithmetic  193 us (21%)
  blocking collectives  164 us (18%)
  local copies, waits for them, and re-layouts  131 us (14%)
  matrix products  103 us (11%)
  between operations  14 us (2%)
    all_to_all x1, blocking collectives, per_device(): lax.all_to_all(outgoing, ('ctx', 'head'), split_axis=0, concat_axis=0, ti...  164 us
    all_to_all x1, waiting for transfers between devices, per_device(): lax.all_to_all(answered, ('ctx', 'head'), split_axis=0, concat_axis=0, ti...  163 us
    another operation x4, other arithmetic, block_setup(): lax.linalg.triangular_solve(system, stacked, left_side=True, lower=True,...  159 us
    all_gather x2, waiting for transfers between devices, carried_in_2(): lax.all_gather(part.astype(kind), axis)  147 us
    dot_general x40, matrix products, batched(): return jnp.einsum('hij,hjk->hik', left, right, precision=HIGHEST)  66.7 us
    gather x10, local copies, waits for them, and re-layouts, per_device(): result_rows[chosen_slots[:, column]].astype(jnp.float32)  59.7 us
  transfers between devices with their start and end apart: 5, of which 3 were waited for; matrix products, arithmetic and copies ran while one was open for 3% of the time, Pallas kernels for 0%

commit v1 on v0

v1 whole, which is shorter than its diff:
```python
import functools

import jax
import jax.numpy as jnp
from jax import lax
from jax.experimental import pallas as pl
from jax.experimental.pallas import tpu as pltpu
from jax.sharding import PartitionSpec as P

DK = 128
DV = 128
PAD = 16
EPS = 1e-06
NN = (((1,), (0,)), ((), ()))
NT = (((1,), (1,)), ((), ()))
TN = (((0,), (0,)), ((), ()))
VMEM_MOST = 56 * 1024 * 1024


def dot16(left, right, dims=NN):
    return lax.dot_general(
        left.astype(jnp.bfloat16),
        right.astype(jnp.bfloat16),
        dims,
        preferred_element_type=jnp.float32,
    )


def halves(x):
    high = x.astype(jnp.bfloat16)
    return high, (x - high.astype(jnp.float32)).astype(jnp.bfloat16)


def dot_split(left, right, dims=NN):
    lh, ll = halves(left)
    rh, rl = halves(right)
    return dot16(lh, rh, dims) + (dot16(lh, rl, dims) + dot16(ll, rh, dims))


def silu(x):
    return x * (1.0 / (1.0 + jnp.exp(-x)))


def filtered(raw_ref, taps_ref, match, lanes):
    rows = raw_ref.shape[0] - PAD
    source = raw_ref[:, lanes].astype(jnp.float32)
    taps = taps_ref[:, lanes]
    total = taps[0:1] * source[PAD:]
    for lag in range(1, taps_ref.shape[0]):
        total = total + taps[lag : lag + 1] * (source[PAD - lag : PAD - lag + rows] * match[lag])
    return silu(total)


def unit_rows(x):
    return x * lax.rsqrt(jnp.sum(x * x, axis=-1, keepdims=True) + EPS)


def inverse_unit_lower(coupling, row, col):
    size = coupling.shape[0]
    apart = row ^ col
    inverse = jnp.where(row == col, 1.0, 0.0) - jnp.where(apart == 1, coupling, 0.0)
    step = 2
    while step < size:
        cross = jnp.where((apart >= step) & (apart < 2 * step), coupling, 0.0)
        inverse = inverse - dot16(inverse, dot16(cross, inverse))
        step *= 2
    return inverse


def local_kernel(
    q_ref, k_ref, v_ref, qt_ref, kt_ref, vt_ref, seg_ref, segrow_ref,
    cum_ref, cumrow_ref, beta_ref, qeff_ref, off_ref, maps_ref,
):
    rows = qeff_ref.shape[1]
    seg = seg_ref[...]
    match = [None] + [(seg[:, lag : lag + 1] == seg[:, 0:1]).astype(jnp.float32) for lag in range(1, 4)]
    ids = seg[:, 0:1]
    carried = (ids == seg_ref[0:1, 1:2]).astype(jnp.float32)
    at_end = (ids == seg_ref[rows - 1 : rows, 0:1]).astype(jnp.float32)
    row = lax.broadcasted_iota(jnp.int32, (rows, rows), 0)
    col = lax.broadcasted_iota(jnp.int32, (rows, rows), 1)
    same = ids == segrow_ref[...]
    causal = (row >= col) & same
    strictly = (row > col) & same
    queries = unit_rows(filtered(q_ref, qt_ref, match, slice(None))) * DK ** (-0.5)
    keys = unit_rows(filtered(k_ref, kt_ref, match, slice(None)))
    q16 = queries.astype(jnp.bfloat16)
    k16 = keys.astype(jnp.bfloat16)
    gram = dot16(k16, k16, NT)
    cross = dot16(q16, k16, NT)
    k32 = k16.astype(jnp.float32)
    q32 = q16.astype(jnp.float32)
    eye = (
        lax.broadcasted_iota(jnp.int32, (DK, DK), 0) == lax.broadcasted_iota(jnp.int32, (DK, DK), 1)
    ).astype(jnp.float32)
    for member in range(qeff_ref.shape[0]):
        lanes = slice(member * DV, (member + 1) * DV)
        values = filtered(v_ref, vt_ref, match, lanes)
        cum = cum_ref[member]
        beta = beta_ref[member]
        decay = jnp.exp(jnp.where(causal, cum - cumrow_ref[member], 0.0))
        coupling = jnp.where(strictly, gram * decay * beta, 0.0)
        within = jnp.where(causal, cross * decay, 0.0)
        grown = jnp.exp(cum) * carried
        inverse = inverse_unit_lower(coupling, row, col)
        stacked = jnp.concatenate([values * beta, k32 * (beta * grown)], axis=1)
        solved = dot16(inverse, stacked)
        both = dot16(within, solved)
        off_ref[member] = both[:, :DV]
        qeff_ref[member] = (q32 * grown - both[:, DV:]).astype(jnp.bfloat16)
        final = cum[rows - 1 : rows]
        weighted = k32 * (at_end * jnp.exp(final - cum))
        sums = dot16(solved, weighted, TN)
        shift_t = sums[:DV]
        forward = (jnp.exp(final) * carried[rows - 1 : rows]) * eye - sums[DV:].T
        for half in range(2):
            at = member * 2 + half
            maps_ref[at, :DK, :] = forward.astype(jnp.bfloat16)
            maps_ref[at, DK:, :] = shift_t[half * (DV // 2) : (half + 1) * (DV // 2)].astype(jnp.bfloat16)


def local_maps(pair, value, pair_taps, value_taps, seg, segrow, cum, cumrow, beta):
    heads, rows = beta.shape[:2]
    key_heads = pair.shape[1] // (2 * DK)
    per = heads // key_heads
    padded = pair.shape[0]
    taps = pair_taps.shape[0]
    whole = lambda g: (0, 0)
    return pl.pallas_call(
        local_kernel,
        grid=(key_heads,),
        in_specs=[
            pl.BlockSpec((padded, DK), lambda g: (0, g)),
            pl.BlockSpec((padded, DK), lambda g: (0, key_heads + g)),
            pl.BlockSpec((padded, per * DV), lambda g: (0, g)),
            pl.BlockSpec((taps, DK), lambda g: (0, g)),
            pl.BlockSpec((taps, DK), lambda g: (0, key_heads + g)),
            pl.BlockSpec((taps, per * DV), lambda g: (0, g)),
            pl.BlockSpec((rows, taps), whole),
            pl.BlockSpec((1, rows), whole),
            pl.BlockSpec((per, rows, 1), lambda g: (g, 0, 0)),
            pl.BlockSpec((per, 1, rows), lambda g: (g, 0, 0)),
            pl.BlockSpec((per, rows, 1), lambda g: (g, 0, 0)),
        ],
        out_specs=[
            pl.BlockSpec((per, rows, DK), lambda g: (g, 0, 0)),
            pl.BlockSpec((per, rows, DV), lambda g: (g, 0, 0)),
            pl.BlockSpec((2 * per, DK + DV // 2, DK), lambda g: (g, 0, 0)),
        ],
        out_shape=[
            jax.ShapeDtypeStruct((heads, rows, DK), jnp.bfloat16),
            jax.ShapeDtypeStruct((heads, rows, DV), jnp.float32),
            jax.ShapeDtypeStruct((2 * heads, DK + DV // 2, DK), jnp.bfloat16),
        ],
        compiler_params=pltpu.CompilerParams(vmem_limit_bytes=VMEM_MOST),
        name="local_maps",
    )(pair, pair, value, pair_taps, pair_taps, value_taps, seg, segrow, cum, cumrow, beta)


def carry_kernel(maps_ref, states_ref):
    state = jnp.zeros(states_ref.shape[1:], jnp.float32)
    for at in range(maps_ref.shape[0]):
        states_ref[at] = state.astype(jnp.bfloat16)
        if at + 1 < maps_ref.shape[0]:
            moved = dot16(state, maps_ref[at, :DK, :], NT)
            state = moved + maps_ref[at, DK:, :].astype(jnp.float32)


def carried_states(maps):
    peers = maps.shape[0]
    return pl.pallas_call(
        carry_kernel,
        out_shape=jax.ShapeDtypeStruct((peers, DV // 2, DK), jnp.bfloat16),
        compiler_params=pltpu.CompilerParams(vmem_limit_bytes=VMEM_MOST),
        name="carried_states",
    )(maps)


def emit_kernel(qeff_ref, off_ref, state_ref, gate_ref, gain_ref, weight_ref, out_ref, gated_ref):
    heads = qeff_ref.shape[0]
    gain = gain_ref[...]
    for head in range(heads):
        lanes = slice(head * DV, (head + 1) * DV)
        mixed = off_ref[head] + dot16(qeff_ref[head], state_ref[head], NT)
        scale = lax.rsqrt(jnp.mean(mixed * mixed, axis=-1, keepdims=True) + EPS)
        gate = silu(gate_ref[:, lanes].astype(jnp.float32))
        gated_ref[:, lanes] = (mixed * scale * gain * gate).astype(jnp.bfloat16)
    width = out_ref.shape[1]
    tile = 512
    for at in range(0, width, tile):
        out_ref[:, at : at + tile] = jnp.dot(
            gated_ref[...], weight_ref[:, at : at + tile], preferred_element_type=jnp.float32
        )


def emitted_rows(qeff, off, states, gate_raw, gain, weight):
    rows, channels = gate_raw.shape
    return pl.pallas_call(
        emit_kernel,
        out_shape=jax.ShapeDtypeStruct((rows, weight.shape[1]), jnp.float32),
        scratch_shapes=[pltpu.VMEM((rows, channels), jnp.bfloat16)],
        compiler_params=pltpu.CompilerParams(vmem_limit_bytes=VMEM_MOST),
        name="emitted_rows",
    )(qeff, off, states, gate_raw, gain, weight)


def mixer(
    pair_raw, value_raw, gate_raw, write_strength, log_decay, segment_ids,
    pair_filter, value_filter, norm_gain, out_weight,
):
    rows = pair_raw.shape[0]
    taps = value_filter.shape[0]
    peers = lax.axis_size("ctx")
    pair = pair_raw.reshape(rows, -1)
    width = pair.shape[1]
    rim = jnp.concatenate([pair[rows - PAD :], value_raw[rows - PAD :]], axis=1)
    before = lax.ppermute(rim, "ctx", [(i, i + 1) for i in range(peers - 1)])
    first = lax.axis_index("ctx") * rows
    padded_ids = jnp.concatenate([jnp.full((taps - 1,), -1, jnp.int32), segment_ids])
    ids = lax.dynamic_slice_in_dim(padded_ids, first, rows + taps - 1)
    seg = jnp.stack([ids[taps - 1 - lag : taps - 1 - lag + rows] for lag in range(taps)], axis=1)
    segrow = ids[taps - 1 :][None, :]
    cum = jnp.cumsum(log_decay, axis=0).T
    qeff, off, maps = local_maps(
        jnp.concatenate([before[:, :width], pair]),
        jnp.concatenate([before[:, width:], value_raw]),
        pair_filter.reshape(taps, -1),
        value_filter,
        seg,
        segrow,
        cum[:, :, None],
        cum[:, None, :],
        write_strength.T[:, :, None],
    )
    heads = qeff.shape[0]
    arrived = lax.all_to_all(maps, "ctx", split_axis=0, concat_axis=0, tiled=True)
    states = lax.all_to_all(carried_states(arrived), "ctx", split_axis=0, concat_axis=0, tiled=True)
    states = states.reshape(heads, DV, DK)
    return emitted_rows(qeff, off, states, gate_raw, norm_gain[None, :], out_weight)


def post_norm(hidden, post_gain):
    hidden_full = hidden.astype(jnp.float32)
    square_mean = jnp.mean(hidden_full * hidden_full, axis=-1, keepdims=True)
    return (hidden_full / jnp.sqrt(square_mean + 1e-06) * post_gain).astype(jnp.bfloat16)


def expert_apply_rows(rows_in, up_matrix, down_matrix):
    hidden_units = down_matrix.shape[0]
    gate_up = jnp.dot(rows_in, up_matrix, preferred_element_type=jnp.float32)
    activated = (jax.nn.silu(gate_up[:, :hidden_units]) * gate_up[:, hidden_units:]).astype(
        jnp.bfloat16
    )
    return jnp.dot(activated, down_matrix, preferred_element_type=jnp.float32).astype(jnp.bfloat16)


def expert_apply(arrived, expert_up, expert_down):
    member_rows = arrived[:, 0]
    flattened = member_rows.reshape(-1, member_rows.shape[-1])
    result = expert_apply_rows(flattened, expert_up[0], expert_down[0])
    outputs = [result.reshape(member_rows.shape)]
    return jnp.stack(outputs, axis=1)


def route_slots(routes, experts_all, capacity):
    assigned = routes.reshape(-1)
    expert_ids = jnp.arange(experts_all, dtype=jnp.int32)
    onehot = (assigned[:, None] == expert_ids[None, :]).astype(jnp.int32)
    slot_rank = jnp.sum((jnp.cumsum(onehot, axis=0) - 1) * onehot, axis=1)
    return assigned * capacity + slot_rank


def per_device(
    pair_raw,
    value_raw,
    gate_raw,
    write_strength,
    log_decay,
    segment_ids,
    pair_filter,
    value_filter,
    norm_gain,
    out_weight,
    residual,
    post_gain,
    routes,
    route_weights,
    expert_up,
    expert_down,
):
    partial = mixer(
        pair_raw, value_raw, gate_raw, write_strength, log_decay, segment_ids,
        pair_filter, value_filter, norm_gain, out_weight,
    )
    half = partial.shape[0] // 2
    core = lax.axis_index("head")
    mine = lax.dynamic_slice_in_dim(partial, core * half, half)
    theirs = lax.dynamic_slice_in_dim(partial, (1 - core) * half, half).astype(jnp.bfloat16)
    attention = mine + lax.ppermute(theirs, "head", [(0, 1), (1, 0)]).astype(jnp.float32)
    hidden = (residual.astype(jnp.float32) + attention).astype(jnp.bfloat16)
    expert_in = post_norm(hidden, post_gain)
    devices_all = lax.axis_size("ctx") * lax.axis_size("head")
    local_experts = expert_up.shape[0]
    experts_all = devices_all * local_experts
    local_rows = routes.shape[0]
    top_count = routes.shape[1]
    capacity = local_rows * top_count * 5 // (4 * experts_all)
    slot_index = route_slots(routes, experts_all, capacity)
    owners = jnp.arange(local_rows * top_count, dtype=jnp.int32) // top_count + 1
    owner_table = jnp.zeros((experts_all * capacity,), jnp.int32).at[slot_index].set(owners)
    filled = owner_table > 0
    outgoing = jnp.where(
        filled[:, None], expert_in[jnp.maximum(owner_table - 1, 0)], jnp.zeros((), jnp.bfloat16)
    )
    outgoing = outgoing.reshape(devices_all, local_experts, capacity, expert_in.shape[1])
    answered = expert_apply(
        lax.all_to_all(outgoing, ("ctx", "head"), split_axis=0, concat_axis=0, tiled=True),
        expert_up,
        expert_down,
    )
    returned = lax.all_to_all(answered, ("ctx", "head"), split_axis=0, concat_axis=0, tiled=True)
    result_rows = returned.reshape(-1, expert_in.shape[1])
    chosen_slots = slot_index.reshape(local_rows, top_count)
    combined = hidden.astype(jnp.float32)
    for column in range(top_count):
        combined = combined + route_weights[:, column : column + 1] * result_rows[
            chosen_slots[:, column]
        ].astype(jnp.float32)
    return combined.astype(jnp.bfloat16)


def solution(mesh):
    return jax.shard_map(
        per_device,
        mesh=mesh,
        in_specs=(
            P(("group", "ctx"), None, "head"),
            P(("group", "ctx"), "head"),
            P(("group", "ctx"), "head"),
            P(("group", "ctx"), "head"),
            P(("group", "ctx"), "head"),
            P("group"),
            P(None, None, "head"),
            P(None, "head"),
            P(),
            P("head", None),
            P(("group", "ctx", "head"), None),
            P(),
            P(("group", "ctx", "head"), None),
            P(("group", "ctx", "head"), None),
            P(("ctx", "head"), None, None),
            P(("ctx", "head"), None, None),
        ),
        out_specs=P(("group", "ctx", "head"), None),
        check_vma=False,
    )
```

time: 932 us -> 568 us (0.61)
  other arithmetic: 193 us -> 23.2 us
  waiting for transfers between devices: 309 us -> 176 us
  matrix products: 103 us -> 15.8 us
  Pallas kernels: 0 us -> 38.5 us
  between operations: 14 us -> 0.78 us
  starting transfers between devices: 9.28 us -> 19.7 us
  local copies, waits for them, and re-layouts: 131 us -> 121 us
    another operation x7, other arithmetic: 169 us -> 10.6 us  [the longest x4 159 us: block_setup(): lax.linalg.triangular_solve(system, stacked, left_side=True, lower=True,...]
    all_gather x2 -> x0, waiting for transfers between devices: 147 us -> none  [carried_in_2(): lax.all_gather(part.astype(kind), axis)]
    dot_general x45 -> x0, matrix products: 85.2 us -> none  [the longest x40 66.7 us: batched(): return jnp.einsum('hij,hjk->hik', left, right, precision=HIGHEST)]
    pallas_call x0 -> x3, Pallas kernels: none -> 38.5 us  [the longest x1 28.8 us: local_maps(): pl.pallas_call(local_kernel, grid=(key_heads,), in_specs=[pl.BlockSpec((p...]
    all_to_all x0 -> x2, waiting for transfers between devices: none -> 12 us  [the longest x1 9.39 us: mixer(): lax.all_to_all(maps, 'ctx', split_axis=0, concat_axis=0, tiled=True)]
    all_to_all x0 -> x2, starting transfers between devices: none -> 10.8 us  [the longest x1 5.93 us: mixer(): lax.all_to_all(maps, 'ctx', split_axis=0, concat_axis=0, tiled=True)]
  transfers between devices with their start and end apart: 5 -> 5, of which waited for: 3 -> 4; matrix products, arithmetic and copies ran while one was open for 3% -> 5% of each run, Pallas kernels for 0% -> 0%
where the time goes in v1:
time: 568 us; the launch traced here: 560 us
  waiting for transfers between devices  176 us (31%)
  blocking collectives  164 us (29%)
  local copies, waits for them, and re-layouts  121 us (21%)
  Pallas kernels  38.5 us (7%)
  other arithmetic  23.2 us (4%)
  starting transfers between devices  19.7 us (3%)
  matrix products  15.8 us (3%)
    all_to_all x1, blocking collectives, per_device(): lax.all_to_all(outgoing, ('ctx', 'head'), split_axis=0, concat_axis=0, ti...  164 us
    all_to_all x1, waiting for transfers between devices, per_device(): lax.all_to_all(answered, ('ctx', 'head'), split_axis=0, concat_axis=0, ti...  163 us
    gather x10, local copies, waits for them, and re-layouts, per_device(): result_rows[chosen_slots[:, column]].astype(jnp.float32)  58.9 us
    pallas_call x1, Pallas kernels, local_maps(): pl.pallas_call(local_kernel, grid=(key_heads,), in_specs=[pl.BlockSpec((p...  28.8 us
    gather x2, local copies, waits for them, and re-layouts, per_device(): expert_in[jnp.maximum(owner_table - 1, 0)]  16.4 us
  transfers between devices with their start and end apart: 5, of which 4 were waited for; matrix products, arithmetic and copies ran while one was open for 5% of the time, Pallas kernels for 0%

profile of v1, /device:TPU:0, one launch (start us, length us, event | category | flops | bytes accessed | tf_op | source)
XLA Modules:
  0.0 559.7 jit_solution(18427294995993752825)
XLA Ops:
  0.0 0.9 slice.106
  1.0 0.8 slice.108
  1.7 4.8 collective-permute-start
  6.6 1.3 reduce-window.14
  7.8 0.2 slice_reduce_fusion
  8.0 0.1 fusion.44
  8.2 0.8 pad_dynamic-slice_fusion
  9.0 0.1 fusion.42
  9.0 0.6 copy.43
  9.6 1.3 copy.56
  11.0 0.8 copy.44.seg_ref
  11.8 1.1 copy.55
  12.9 1.4 copy.45.cum_ref
  14.3 2.1 copy.46.beta_ref
  16.4 2.1 pad_maximum_fusion
  18.5 28.8 %local_maps.1 = (bf16[8,256,128]{2,1,0:T(8,128)(2,1)}, f32[8,256,128]{2,1,0:T(8,128)}, bf16[16,192,128]{2,1,0:T(8,128)(2,1)}) custom-call(bf16[272,1024]{1,0:T(8,128)(2,1)} %get-tuple-element.41.q_ref.k_ref, bf16[272,1024]{1,0:T(8,128)(2,1)} %get-tuple-element.41.q_ref.k_ref, bf16[272,1024]{1,0:T(8,128)(2,1)} %get-tuple-element.42.v_ref, ...), custom_call_target="tpu_custom_call" | custom-call | tf_op jit(solution)/shard_map/local_maps/pallas_call | solution.py:129
  47.2 5.9 %all-to-all-start = ((bf16[16,192,128]{2,1,0:T(8,128)(2,1)}), bf16[16,192,128]{2,1,0:T(8,128)(2,1)S(1)}, u32[]{:S(2)}, u32[]{:S(2)}) async-start(bf16[16,192,128]{2,1,0:T(8,128)(2,1)} %get-tuple-element.10), calls=%async_computation | async-start | bytes 1572864 | tf_op jit(solution)/shard_map/all_to_all | solution.py:236
  53.2 0.1 copy.47
  53.3 0.1 eq.29
  53.4 0.1 eq.25
  53.6 9.1 %reduce-window.16 = s32[32,10,128]{2,1,0:T(8,128)S(1)} reduce-window(s32[32,10,128]{2,1,0:T(8,128)S(1)} %fusion.19, s32[]{:T(128)} %constant.21.clone.1), window={size=1x1x128 pad=0_0x0_0x127_0}, to_apply=%region_2.3 | reduce-window | flops 5201920 | bytes 327684 | tf_op jit(solution)/shard_map/reduce-window.2
  62.7 0.1 slice.166
  62.8 0.2 copy.50
  63.0 0.1 copy.51
  63.1 0.1 add_add_fusion
  63.3 9.4 %all-to-all-done.maps_ref = bf16[16,192,128]{2,1,0:T(8,128)(2,1)S(1)} async-done(((bf16[16,192,128]{2,1,0:T(8,128)(2,1)}), bf16[16,192,128]{2,1,0:T(8,128)(2,1)S(1)}, u32[]{:S(2)}, u32[]{:S(2)}) %all-to-all-start) | async-done | bytes 786464 | tf_op jit(solution)/shard_map/all_to_all | solution.py:236
  72.7 0.9 copy-done.1
  73.5 3.6 carried_states.1
  77.2 4.9 all-to-all-start.1
  82.1 0.1 fusion.21
  82.2 0.1 reduce_sum.25
  82.3 0.1 mul.154
  82.5 5.4 scatter_custom_fusion
  88.0 2.6 all-to-all-done.1
  90.6 0.7 copy-done.2
  91.3 6.1 %emitted_rows.1 = f32[256,2048]{1,0:T(8,128)} custom-call(bf16[8,256,128]{2,1,0:T(8,128)(2,1)} %get-tuple-element.8.qeff_ref, f32[8,256,128]{2,1,0:T(8,128)} %get-tuple-element.9.off_ref, bf16[8,128,128]{2,1,0:T(8,128)(2,1)} %bitcast.70, bf16[256,1024]{1,0:T(8,128)(2,1)} %gate_ref.1, f32[1,128]{1,0:T(1,128)} %bitcast.88, bf16[1024,2048]{1,0:T(8,128)(2,1)} %weight_ref.1), custom_call_target="tpu_custom_call" | custom-call | tf_op jit(solution)/shard_map/emitted_rows/pallas_call | solution.py:198
  97.4 1.3 dynamic-slice_convert_fusion
  98.8 0.1 broadcast_in_dim.25
  98.9 1.7 collective-permute-done.1
  100.6 1.7 fusion.6
  102.3 0.2 fusion.8
  102.5 7.7 %gather_fusion = bf16[1600,2048]{1,0:T(8,128)(2,1)} fusion(bf16[128,2048]{1,0:T(8,128)(2,1)S(1)} %fusion.8, s32[2048]{0:T(1024)S(1)} %pad_clamp_fusion), kind=kCustom, calls=%fused_computation | custom fusion | bytes 13113600 | tf_op jit(solution)/shard_map/gather | solution.py:313
  110.2 8.7 %gather.36 = bf16[32,1,50,2048]{3,2,0,1:T(8,128)(2,1)} reshape(bf16[1600,2048]{1,0:T(8,128)(2,1)} %gather_fusion) | data formatting | bytes 13107200 | tf_op jit(solution)/shard_map/gather | solution.py:313
  118.9 3.7 select_bitcast_fusion
  122.6 164.2 %all_to_all.20 = bf16[32,1,50,2048]{3,2,1,0:T(8,128)(2,1)} all-to-all(bf16[32,1,50,2048]{3,2,1,0:T(8,128)(2,1)S(1)} %select_bitcast_fusion), channel_id=1, replica_groups=mesh['group'=1,'ctx'=16,'head'=2] {'ctx','head'}, dimensions={0} | all-to-all | bytes 13107200 | tf_op jit(solution)/shard_map/all_to_all | solution.py:317
  286.8 8.8 %reshape_squeeze.3 = bf16[1600,2048]{1,0:T(8,128)(2,1)} reshape(bf16[32,1,50,2048]{3,2,1,0:T(8,128)(2,1)} %all_to_all.20) | data formatting | bytes 13107200 | tf_op jit(solution)/shard_map/reshape;squeeze | solution.py:259
  295.6 10.3 %fusion = f32[1600,1024]{1,0:T(8,128)S(1)} fusion(bf16[1600,2048]{1,0:T(8,128)(2,1)} %reshape_squeeze.3, bf16[1,2048,1024]{2,1,0:T(8,128)(2,1)} %param.30), kind=kOutput, calls=%fused_computation.14 | convolution fusion | flops 6710886400 | bytes 17301504 | tf_op jit(solution)/shard_map/dot_general | solution.py:250
  305.9 5.5 convolution_convert_fusion
  311.4 8.7 %stack_reshape.3 = bf16[32,1,50,2048]{3,2,0,1:T(8,128)(2,1)} reshape(bf16[1600,2048]{1,0:T(8,128)(2,1)} %convolution_convert_fusion) | data formatting | bytes 13107200 | tf_op jit(solution)/shard_map/stack;reshape | solution.py:262
  320.1 3.9 all-to-all-start.3
  324.0 0.4 fusion.22
  324.6 162.6 %all-to-all-done.3 = bf16[32,1,50,2048]{3,2,1,0:T(8,128)(2,1)} async-done(((bf16[32,1,50,2048]{3,2,1,0:T(8,128)(2,1)}), bf16[32,1,50,2048]{3,2,1,0:T(8,128)(2,1)}, u32[]{:S(2)}, u32[]{:S(2)}) %all-to-all-start.3) | async-done | bytes 6553632 | tf_op jit(solution)/shard_map/all_to_all | solution.py:321
  487.1 9.0 %reshape.145 = bf16[1600,2048]{1,0:T(8,128)(2,1)} reshape(bf16[32,1,50,2048]{3,2,1,0:T(8,128)(2,1)} %all-to-all-done.3) | data formatting | bytes 13107200 | tf_op jit(solution)/shard_map/reshape | solution.py:322
  496.1 5.1 gather_fusion.10
  501.3 5.9 %gather_fusion.9 = bf16[128,2048]{1,0:T(8,128)(2,1)} fusion(bf16[1600,2048]{1,0:T(8,128)(2,1)} %reshape.145, s32[1024]{0:T(1024)S(1)} %get-tuple-element.44), kind=kCustom, calls=%fused_computation.9 | custom fusion | bytes 1049088 | tf_op jit(solution)/shard_map/gather | solution.py:326
  507.2 5.9 %gather_fusion.8 = bf16[128,2048]{1,0:T(8,128)(2,1)} fusion(bf16[1600,2048]{1,0:T(8,128)(2,1)} %reshape.145, s32[1024]{0:T(1024)S(1)} %get-tuple-element.45), kind=kCustom, calls=%fused_computation.8 | custom fusion | bytes 1049088 | tf_op jit(solution)/shard_map/gather | solution.py:326
  513.1 6.0 %gather_fusion.7 = bf16[128,2048]{1,0:T(8,128)(2,1)} fusion(bf16[1600,2048]{1,0:T(8,128)(2,1)} %reshape.145, s32[1024]{0:T(1024)S(1)} %get-tuple-element.46), kind=kCustom, calls=%fused_computation.7 | custom fusion | bytes 1049088 | tf_op jit(solution)/shard_map/gather | solution.py:326
  519.1 6.0 %gather_fusion.6 = bf16[128,2048]{1,0:T(8,128)(2,1)} fusion(bf16[1600,2048]{1,0:T(8,128)(2,1)} %reshape.145, s32[1024]{0:T(1024)S(1)} %get-tuple-element.47), kind=kCustom, calls=%fused_computation.6 | custom fusion | bytes 1049088 | tf_op jit(solution)/shard_map/gather | solution.py:326
  525.0 6.0 %gather_fusion.5 = bf16[128,2048]{1,0:T(8,128)(2,1)} fusion(bf16[1600,2048]{1,0:T(8,128)(2,1)} %reshape.145, s32[1024]{0:T(1024)S(1)} %get-tuple-element.48), kind=kCustom, calls=%fused_computation.5 | custom fusion | bytes 1049088 | tf_op jit(solution)/shard_map/gather | solution.py:326
  531.0 6.2 %gather_fusion.4 = bf16[128,2048]{1,0:T(8,128)(2,1)} fusion(bf16[1600,2048]{1,0:T(8,128)(2,1)} %reshape.145, s32[1024]{0:T(1024)S(1)} %get-tuple-element.49), kind=kCustom, calls=%fused_computation.4 | custom fusion | bytes 1049088 | tf_op jit(solution)/shard_map/gather | solution.py:326
  537.2 6.0 %gather_fusion.3 = bf16[128,2048]{1,0:T(8,128)(2,1)} fusion(bf16[1600,2048]{1,0:T(8,128)(2,1)} %reshape.145, s32[1024]{0:T(1024)S(1)} %get-tuple-element.50), kind=kCustom, calls=%fused_computation.3 | custom fusion | bytes 1049088 | tf_op jit(solution)/shard_map/gather | solution.py:326
  543.1 5.9 %gather_fusion.2 = bf16[128,2048]{1,0:T(8,128)(2,1)} fusion(bf16[1600,2048]{1,0:T(8,128)(2,1)} %reshape.145, s32[1024]{0:T(1024)S(1)} %get-tuple-element.51), kind=kCustom, calls=%fused_computation.2 | custom fusion | bytes 1049088 | tf_op jit(solution)/shard_map/gather | solution.py:326
  549.1 6.0 %gather_fusion.1 = bf16[128,2048]{1,0:T(8,128)(2,1)} fusion(bf16[1600,2048]{1,0:T(8,128)(2,1)} %reshape.145, s32[1024]{0:T(1024)S(1)} %get-tuple-element.52), kind=kCustom, calls=%fused_computation.1 | custom fusion | bytes 1049088 | tf_op jit(solution)/shard_map/gather | solution.py:326
  555.0 4.3 fusion.18
  (36 shorter events, 0.4 us)
Async XLA Ops:
  0.0 305.9 %copy-start = (bf16[1,512,2048]{2,1,0:T(8,128)(2,1)S(1)}, bf16[1,512,2048]{2,1,0:T(8,128)(2,1)}, u32[]{:S(2)}) copy-start(bf16[1,512,2048]{2,1,0:T(8,128)(2,1)} %param.31) | copy-start | bytes 6291460
  0.0 53.2 %copy-start.5 = (s32[128,10]{0,1:T(8,128)S(1)}, s32[128,10]{0,1:T(8,128)}, u32[]{:S(2)}) copy-start(s32[128,10]{0,1:T(8,128)} %param.28) | copy-start | bytes 15364
  1.7 14.6 %collective-permute-start = (bf16[16,2048]{1,0:T(8,128)(2,1)S(1)}, bf16[16,2048]{1,0:T(8,128)(2,1)S(1)}, u32[]{:S(2)}, u32[]{:S(2)}) collective-permute-start(bf16[16,2048]{1,0:T(8,128)(2,1)S(1)} %pad_maximum_fusion.2), channel_id=1, source_target_pairs={{0,2},{2,4},{4,6},{6,8},{8,10},{10,12},{12,14},{14,16},{16,18},{18... | collective-permute-start | bytes 196616 | tf_op jit(solution)/shard_map/ppermute | solution.py:217
  9.0 9.4 %copy-start.3 = (s32[256]{0:T(256)}, s32[256]{0:T(256)S(1)}, u32[]{:S(2)}) copy-start(s32[256]{0:T(256)S(1)} %get-tuple-element.37) | copy-start | bytes 3076
  47.2 25.4 %all-to-all-start = ((bf16[16,192,128]{2,1,0:T(8,128)(2,1)}), bf16[16,192,128]{2,1,0:T(8,128)(2,1)S(1)}, u32[]{:S(2)}, u32[]{:S(2)}) async-start(bf16[16,192,128]{2,1,0:T(8,128)(2,1)} %get-tuple-element.10), calls=%async_computation | async-start | bytes 1572864 | tf_op jit(solution)/shard_map/all_to_all | solution.py:236
  72.7 0.9 copy-start.1
  77.2 13.4 %all-to-all-start.1 = ((bf16[16,64,128]{2,1,0:T(8,128)(2,1)}), bf16[16,64,128]{2,1,0:T(8,128)(2,1)S(1)}, u32[]{:S(2)}, u32[]{:S(2)}) async-start(bf16[16,64,128]{2,1,0:T(8,128)(2,1)} %carried_states.1), calls=%async_computation.1 | async-start | bytes 524288 | tf_op jit(solution)/shard_map/all_to_all | solution.py:237
  82.1 20.2 %copy-start.4 = (f32[2048]{0:T(1024)S(1)}, f32[2048]{0:T(1024)}, u32[]{:S(2)}) copy-start(f32[2048]{0:T(1024)} %param.27) | copy-start | bytes 24580
  90.6 0.7 copy-start.2
  98.7 2.0 collective-permute-start.1
  320.1 4.5 copy-start.6
  320.1 167.1 %all-to-all-start.3 = ((bf16[32,1,50,2048]{3,2,1,0:T(8,128)(2,1)}), bf16[32,1,50,2048]{3,2,1,0:T(8,128)(2,1)}, u32[]{:S(2)}, u32[]{:S(2)}) async-start(bf16[32,1,50,2048]{3,2,1,0:T(8,128)(2,1)} %bitcast.68), calls=%async_computation.3 | async-start | bytes 14680064 | tf_op jit(solution)/shard_map/all_to_all | solution.py:321

commit v2 on v1

--- a/solution.py
+++ b/solution.py
@@ -238,36 +238,271 @@
     states = states.reshape(heads, DV, DK)
     return emitted_rows(qeff, off, states, gate_raw, norm_gain[None, :], out_weight)
 
+PLANE = 4
+AGZ, AGX, AGY, AGA, AGB, DA, DB, XA, XB, YA, YB, RSZ = range(12)
+
+
+def expert_kernel(
+    x_ref, slot_ref, weight_ref, up_mine, up_other, down_mine, down_other, out_ref,
+    got, part, diag, from_x, from_y, sums, from_z, up, down, rows_in, rows_out, chosen,
+    send_sem, recv_sem, local_sem,
+):
+    planes = got.shape[0] // PLANE
+    tokens = got.shape[1]
+    half = tokens // 2
+    first, second = pl.ds(0, half), pl.ds(half, half)
+    slots = rows_in.shape[0]
+    me = lax.axis_index("ctx")
+    x, y, z = me % 2, (me // 2) % 2, me // PLANE
+    beside_x = me + 1 - 2 * x
+    beside_y = me + 2 - 4 * y
+
+    def plane_of(k):
+        return (z % 2 + k % 2) % 2 + 2 * ((z // 2 + k // 2) % 2)
+
+    def along_z(k):
+        return PLANE * plane_of(k) + 2 * y + x
+
+    def block(k, flip_y, flip_x):
+        row = 1 - y if flip_y else y
+        column = 1 - x if flip_x else x
+        return PLANE * plane_of(k) + 2 * row + column
+
+    def copy(kind, k, source, target, device):
+        return pltpu.make_async_remote_copy(
+            src_ref=source,
+            dst_ref=target,
+            send_sem=send_sem.at[kind, k],
+            recv_sem=recv_sem.at[kind, k],
+            device_id={"ctx": device},
+            device_id_type=pl.DeviceIdType.MESH,
+        )
+
+    def arrived(kind, k, place, device):
+        copy(kind, k, place, place, device).wait_recv()
+
+    loads = [
+        pltpu.make_async_copy(source, target, local_sem.at[at])
+        for at, (source, target) in enumerate(
+            [
+                (up_mine.at[0], up.at[0]),
+                (up_other.at[0], up.at[1]),
+                (down_mine.at[0], down.at[0]),
+                (down_other.at[0], down.at[1]),
+            ]
+        )
+    ]
+    for load in loads:
+        load.start()
+    got[me] = x_ref[...]
+
+    partners = [beside_x, beside_y] + [along_z(k) for k in range(1, planes)]
+    barrier = pltpu.get_barrier_semaphore()
+    for partner in partners:
+        pl.semaphore_signal(
+            barrier, inc=1, device_id={"ctx": partner}, device_id_type=pl.DeviceIdType.MESH
+        )
+    pl.semaphore_wait(barrier, len(partners))
+
+    def share_in_plane(k):
+        own = block(k, False, False)
+        copy(AGX, k, got.at[own], got.at[own], beside_x).start()
+        copy(AGY, k, got.at[own], got.at[own], beside_y).start()
+
+    share_in_plane(0)
+    for k in range(1, planes):
+        copy(AGZ, k, got.at[me], got.at[me], along_z(k)).start()
+    for load in loads:
+        load.wait()
+
+    def experts(k):
+        plane = plane_of(k)
+        base = PLANE * plane
+        slot_rows = slot_ref[plane]
+        weight_rows = weight_ref[plane]
+        place = lax.broadcasted_iota(jnp.int32, (slots, PLANE * tokens), 0)
+        source = got[pl.ds(base, PLANE)].reshape(PLANE * tokens, got.shape[2])
+        for e in range(2):
+            here = place == slot_rows[e : e + 1]
+            pick = jnp.where(here, 1.0, 0.0).astype(jnp.bfloat16)
+            chosen[pl.ds(e * slots, slots), :] = jnp.where(here, weight_rows[e : e + 1], 0.0).astype(
+                jnp.bfloat16
+            )
+            rows_in[...] = jnp.dot(pick, source, preferred_element_type=jnp.float32).astype(
+                jnp.bfloat16
+            )
+            units = jnp.dot(rows_in[...], up[e], preferred_element_type=jnp.float32)
+            width = units.shape[1] // 2
+            active = (silu(units[:, :width]) * units[:, width:]).astype(jnp.bfloat16)
+            rows_out[pl.ds(e * slots, slots), :] = jnp.dot(
+                active, down[e], preferred_element_type=jnp.float32
+            ).astype(jnp.bfloat16)
+        for b in range(PLANE):
+            part[base + b] = lax.dot_general(
+                chosen[:, b * tokens : (b + 1) * tokens],
+                rows_out[...],
+                TN,
+                preferred_element_type=jnp.float32,
+            ).astype(jnp.bfloat16)
+
+    def give_first(k):
+        across, xb, yb = block(k, True, True), block(k, False, True), block(k, True, False)
+        copy(DA, k, part.at[across, first], diag.at[k, first], beside_y).start()
+        copy(DB, k, part.at[across, second], diag.at[k, second], beside_x).start()
+        copy(XB, k, part.at[xb, second], from_x.at[k, second], beside_x).start()
+        copy(YA, k, part.at[yb, first], from_y.at[k, first], beside_y).start()
+
+    def give_second(k):
+        xb, yb = block(k, False, True), block(k, True, False)
+        arrived(DA, k, diag.at[k, first], beside_y)
+        part[xb, first] = (
+            part[xb, first].astype(jnp.float32) + diag[k, first].astype(jnp.float32)
+        ).astype(jnp.bfloat16)
+        copy(XA, k, part.at[xb, first], from_x.at[k, first], beside_x).start()
+        arrived(DB, k, diag.at[k, second], beside_x)
+        part[yb, second] = (
+            part[yb, second].astype(jnp.float32) + diag[k, second].astype(jnp.float32)
+        ).astype(jnp.bfloat16)
+        copy(YB, k, part.at[yb, second], from_y.at[k, second], beside_y).start()
+
+    def plane_sum(k):
+        arrived(XA, k, from_x.at[k, first], beside_x)
+        arrived(XB, k, from_x.at[k, second], beside_x)
+        arrived(YA, k, from_y.at[k, first], beside_y)
+        arrived(YB, k, from_y.at[k, second], beside_y)
+        own = block(k, False, False)
+        return (
+            part[own].astype(jnp.float32)
+            + from_x[k].astype(jnp.float32)
+            + from_y[k].astype(jnp.float32)
+        )
+
+    def give_third(k):
+        sums[k] = plane_sum(k).astype(jnp.bfloat16)
+        copy(RSZ, k, sums.at[k], from_z.at[k], along_z(k)).start()
+
+    def turn(k, unused):
+        across_x, across_y = block(k, False, True), block(k, True, False)
+        arrived(AGX, k, got.at[across_x], beside_x)
+        copy(AGA, k, got.at[across_x, first], got.at[across_x, first], beside_y).start()
+        arrived(AGY, k, got.at[across_y], beside_y)
+        copy(AGB, k, got.at[across_y, second], got.at[across_y, second], beside_x).start()
+
+        @pl.when(k < planes - 1)
+        def _():
+            arrived(AGZ, k + 1, got.at[along_z(k + 1)], along_z(k + 1))
+            share_in_plane(k + 1)
+
+        across = block(k, True, True)
+        arrived(AGA, k, got.at[across, first], beside_y)
+        arrived(AGB, k, got.at[across, second], beside_x)
+        experts(k)
+
+        @pl.when(k >= 1)
+        def _():
+            give_first(k)
+
+        @pl.when(k >= 2)
+        def _():
+            give_second(k - 1)
+
+        @pl.when(k >= 3)
+        def _():
+            give_third(k - 2)
+
+        return unused
+
+    lax.fori_loop(0, planes, turn, 0)
+    give_first(0)
+    give_second(3)
+    give_third(2)
+    give_second(0)
+    give_third(3)
+    total = plane_sum(0)
+    for k in range(1, planes):
+        arrived(RSZ, k, from_z.at[k], along_z(k))
+        total = total + from_z[k].astype(jnp.float32)
+    out_ref[...] = total
+
+    for k in range(planes):
+        for kind in (AGX, AGY):
+            copy(kind, k, got.at[0], got.at[0], beside_x).wait_send()
+        for kind in (AGA, AGB):
+            copy(kind, k, got.at[0, first], got.at[0, first], beside_x).wait_send()
+        for kind in (DA, DB, XA, XB, YA, YB):
+            copy(kind, k, part.at[0, first], diag.at[0, first], beside_x).wait_send()
+        if k > 0:
+            copy(AGZ, k, got.at[0], got.at[0], beside_x).wait_send()
+            copy(RSZ, k, sums.at[0], from_z.at[0], beside_x).wait_send()
+
+
+def expert_sums(x, slot, weight, up_mine, up_other, down_mine, down_other, capacity):
+    peers = lax.axis_size("ctx")
+    planes = peers // PLANE
+    assert planes == 4 and x.shape[0] % 32 == 0
+    tokens, width = x.shape
+    units = up_mine.shape[2]
+    slots = (PLANE * capacity + 15) // 16 * 16
+    vmem = pl.BlockSpec(memory_space=pltpu.VMEM)
+    hbm = pl.BlockSpec(memory_space=pl.ANY)
+    half = jnp.bfloat16
+    return pl.pallas_call(
+        expert_kernel,
+        out_shape=jax.ShapeDtypeStruct((tokens, width), jnp.float32),
+        in_specs=[vmem, vmem, vmem, hbm, hbm, hbm, hbm],
+        out_specs=vmem,
+        scratch_shapes=[
+            pltpu.VMEM((peers, tokens, width), half),
+            pltpu.VMEM((peers, tokens, width), half),
+            pltpu.VMEM((planes, tokens, width), half),
+            pltpu.VMEM((planes, tokens, width), half),
+            pltpu.VMEM((planes, tokens, width), half),
+            pltpu.VMEM((planes, tokens, width), half),
+            pltpu.VMEM((planes, tokens, width), half),
+            pltpu.VMEM((2, width, units), half),
+            pltpu.VMEM((2, units // 2, width), half),
+            pltpu.VMEM((slots, width), half),
+            pltpu.VMEM((2 * slots, width), half),
+            pltpu.VMEM((2 * slots, PLANE * tokens), half),
+            pltpu.SemaphoreType.DMA((12, planes)),
+            pltpu.SemaphoreType.DMA((12, planes)),
+            pltpu.SemaphoreType.DMA((4,)),
+        ],
+        compiler_params=pltpu.CompilerParams(
+            collective_id=0, has_side_effects=True, vmem_limit_bytes=VMEM_MOST
+        ),
+        name="expert_sums",
+    )(x, slot, weight, up_mine, up_other, down_mine, down_other)
+
+
+def route_tables(routes, route_weights):
+    peers, cores = lax.axis_size("ctx"), lax.axis_size("head")
+    experts = jnp.arange(peers * cores, dtype=jnp.int32)
+    named = (routes[None] == experts[:, None, None]).astype(jnp.float32)
+    dense = jnp.sum(named * route_weights[None], axis=2)
+    tokens = routes.shape[0]
+    seen = lax.all_to_all(
+        dense.reshape(peers, cores, tokens), "ctx", split_axis=0, concat_axis=0, tiled=True
+    )
+    seen = jnp.where(lax.axis_index("head") == 0, seen, seen[:, ::-1])
+    seen = seen.reshape(peers // PLANE, PLANE, cores, tokens).swapaxes(1, 2)
+    seen = seen.reshape(peers // PLANE, cores, PLANE * tokens)
+    filled = seen > 0
+    span = PLANE * tokens
+    upto = (
+        lax.broadcasted_iota(jnp.int32, (span, span), 0)
+        <= lax.broadcasted_iota(jnp.int32, (span, span), 1)
+    ).astype(jnp.bfloat16)
+    rank = jnp.dot(
+        filled.reshape(-1, span).astype(jnp.bfloat16), upto, preferred_element_type=jnp.float32
+    ).reshape(seen.shape)
+    return jnp.where(filled, rank.astype(jnp.int32) - 1, -1), seen
+
 
 def post_norm(hidden, post_gain):
     hidden_full = hidden.astype(jnp.float32)
     square_mean = jnp.mean(hidden_full * hidden_full, axis=-1, keepdims=True)
     return (hidden_full / jnp.sqrt(square_mean + 1e-06) * post_gain).astype(jnp.bfloat16)
-
-
-def expert_apply_rows(rows_in, up_matrix, down_matrix):
-    hidden_units = down_matrix.shape[0]
-    gate_up = jnp.dot(rows_in, up_matrix, preferred_element_type=jnp.float32)
-    activated = (jax.nn.silu(gate_up[:, :hidden_units]) * gate_up[:, hidden_units:]).astype(
-        jnp.bfloat16
-    )
-    return jnp.dot(activated, down_matrix, preferred_element_type=jnp.float32).astype(jnp.bfloat16)
-
-
-def expert_apply(arrived, expert_up, expert_down):
-    member_rows = arrived[:, 0]
-    flattened = member_rows.reshape(-1, member_rows.shape[-1])
-    result = expert_apply_rows(flattened, expert_up[0], expert_down[0])
-    outputs = [result.reshape(member_rows.shape)]
-    return jnp.stack(outputs, axis=1)
-
-
-def route_slots(routes, experts_all, capacity):
-    assigned = routes.reshape(-1)
-    expert_ids = jnp.arange(experts_all, dtype=jnp.int32)
-    onehot = (assigned[:, None] == expert_ids[None, :]).astype(jnp.int32)
-    slot_rank = jnp.sum((jnp.cumsum(onehot, axis=0) - 1) * onehot, axis=1)
-    return assigned * capacity + slot_rank
 
 
 def per_device(
@@ -288,6 +523,11 @@
     expert_up,
     expert_down,
 ):
+    swap = [(0, 1), (1, 0)]
+    devices_all = lax.axis_size("ctx") * lax.axis_size("head")
+    up_other = lax.ppermute(expert_up, "head", swap)
+    down_other = lax.ppermute(expert_down, "head", swap)
+    slot, weight = route_tables(routes, route_weights)
     partial = mixer(
         pair_raw, value_raw, gate_raw, write_strength, log_decay, segment_ids,
         pair_filter, value_filter, norm_gain, out_weight,
@@ -296,37 +536,14 @@
     core = lax.axis_index("head")
     mine = lax.dynamic_slice_in_dim(partial, core * half, half)
     theirs = lax.dynamic_slice_in_dim(partial, (1 - core) * half, half).astype(jnp.bfloat16)
-    attention = mine + lax.ppermute(theirs, "head", [(0, 1), (1, 0)]).astype(jnp.float32)
+    attention = mine + lax.ppermute(theirs, "head", swap).astype(jnp.float32)
     hidden = (residual.astype(jnp.float32) + attention).astype(jnp.bfloat16)
     expert_in = post_norm(hidden, post_gain)
-    devices_all = lax.axis_size("ctx") * lax.axis_size("head")
-    local_experts = expert_up.shape[0]
-    experts_all = devices_all * local_experts
-    local_rows = routes.shape[0]
-    top_count = routes.shape[1]
-    capacity = local_rows * top_count * 5 // (4 * experts_all)
-    slot_index = route_slots(routes, experts_all, capacity)
-    owners = jnp.arange(local_rows * top_count, dtype=jnp.int32) // top_count + 1
-    owner_table = jnp.zeros((experts_all * capacity,), jnp.int32).at[slot_index].set(owners)
-    filled = owner_table > 0
-    outgoing = jnp.where(
-        filled[:, None], expert_in[jnp.maximum(owner_table - 1, 0)], jnp.zeros((), jnp.bfloat16)
+    capacity = routes.shape[0] * routes.shape[1] * 5 // (4 * devices_all)
+    answered = expert_sums(
+        expert_in, slot, weight, expert_up, up_other, expert_down, down_other, capacity
     )
-    outgoing = outgoing.reshape(devices_all, local_experts, capacity, expert_in.shape[1])
-    answered = expert_apply(
-        lax.all_to_all(outgoing, ("ctx", "head"), split_axis=0, concat_axis=0, tiled=True),
-        expert_up,
-        expert_down,
-    )
-    returned = lax.all_to_all(answered, ("ctx", "head"), split_axis=0, concat_axis=0, tiled=True)
-    result_rows = returned.reshape(-1, expert_in.shape[1])
-    chosen_slots = slot_index.reshape(local_rows, top_count)
-    combined = hidden.astype(jnp.float32)
-    for column in range(top_count):
-        combined = combined + route_weights[:, column : column + 1] * result_rows[
-            chosen_slots[:, column]
-        ].astype(jnp.float32)
-    return combined.astype(jnp.bfloat16)
+    return (hidden.astype(jnp.float32) + answered).astype(jnp.bfloat16)
 
 
 def solution(mesh):

time: 568 us -> 283 us (0.50)
  Pallas kernels: 38.5 us -> 199 us
  waiting for transfers between devices: 176 us -> 16.3 us
  blocking collectives: 164 us -> 28.1 us
  local copies, waits for them, and re-layouts: 121 us -> 12.7 us
  other arithmetic: 23.2 us -> 7.83 us
  matrix products: 15.8 us -> 0.79 us
  starting transfers between devices: 19.7 us -> 12.2 us
    all_to_all x2 -> x1, waiting for transfers between devices: 172 us -> 7.19 us  [route_tables(): lax.all_to_all(dense.reshape(peers, cores, tokens), 'ctx', split_axis=0,...]
    pallas_call x0 -> x1, Pallas kernels: none -> 161 us  [expert_sums(): pl.pallas_call(expert_kernel, out_shape=jax.ShapeDtypeStruct((tokens, wid...]
    all_to_all x1, blocking collectives: 164 us -> 28.1 us  [mixer(): lax.all_to_all(maps, 'ctx', split_axis=0, concat_axis=0, tiled=True)]
    gather x12 -> x0, local copies, waits for them, and re-layouts: 75.3 us -> none  [the longest x10 58.9 us: per_device(): result_rows[chosen_slots[:, column]].astype(jnp.float32)]
    another operation x8 -> x3, local copies, waits for them, and re-layouts: 19.8 us -> 1.95 us  [the longest x1 8.78 us: expert_apply(): flattened = member_rows.reshape(-1, member_rows.shape[-1])]
    dot_general x2 -> x1, matrix products: 15.8 us -> 0.79 us  [route_tables(): jnp.dot(filled.reshape(-1, span).astype(jnp.bfloat16), upto, preferred_el...]
    another operation x6 -> x4, other arithmetic: 10.5 us -> 1.43 us
    reshape x1 -> x2, local copies, waits for them, and re-layouts: 8.96 us -> 0.63 us  [route_tables(): seen = seen.reshape(peers // PLANE, cores, PLANE * tokens)]
  transfers between devices with their start and end apart: 5 -> 6, of which waited for: 4 -> 2; matrix products, arithmetic and copies ran while one was open for 5% -> 6% of each run, Pallas kernels for 0% -> 14%
where the time goes in v2:
time: 283 us; the launch traced here: 278 us
  Pallas kernels  199 us (70%)
  blocking collectives  28.1 us (10%)
  waiting for transfers between devices  16.3 us (6%)
  local copies, waits for them, and re-layouts  12.7 us (4%)
  starting transfers between devices  12.2 us (4%)
  other arithmetic  7.83 us (3%)
    pallas_call x1, Pallas kernels, expert_sums(): pl.pallas_call(expert_kernel, out_shape=jax.ShapeDtypeStruct((tokens, wid...  161 us
    pallas_call x1, Pallas kernels, local_maps(): pl.pallas_call(local_kernel, grid=(key_heads,), in_specs=[pl.BlockSpec((p...  28.7 us
    all_to_all x1, blocking collectives, mixer(): lax.all_to_all(maps, 'ctx', split_axis=0, concat_axis=0, tiled=True)  28.1 us
    all_to_all x1, waiting for transfers between devices, mixer(): lax.all_to_all(carried_states(arrived), 'ctx', split_axis=0, concat_axis=...  9.12 us
    all_to_all x1, waiting for transfers between devices, route_tables(): lax.all_to_all(dense.reshape(peers, cores, tokens), 'ctx', split_axis=0,...  7.19 us
    pallas_call x1, Pallas kernels, emitted_rows(): pl.pallas_call(emit_kernel, out_shape=jax.ShapeDtypeStruct((rows, weight....  6.12 us
  transfers between devices with their start and end apart: 6, of which 2 were waited for; matrix products, arithmetic and copies ran while one was open for 6% of the time, Pallas kernels for 14%

profile of v2, /device:TPU:0, one launch (start us, length us, event | category | flops | bytes accessed | tf_op | source)
XLA Modules:
  0.0 277.6 jit_solution(11362890775252512938)
XLA Ops:
  0.0 0.0 copy-start.2
  0.0 0.0 copy-start.5
  0.0 0.9 slice.34
  0.9 0.8 slice.36
  1.6 4.8 %collective-permute-start = (bf16[16,2048]{1,0:T(8,128)(2,1)S(1)}, bf16[16,2048]{1,0:T(8,128)(2,1)S(1)}, u32[]{:S(2)}, u32[]{:S(2)}) collective-permute-start(bf16[16,2048]{1,0:T(8,128)(2,1)S(1)} %pad_maximum_fusion.2), channel_id=1, source_target_pairs={{0,2},{2,4},{4,6},{6,8},{8,10},{10,12},{12,14},{14,16},{16,18},{18... | collective-permute-start | bytes 196616 | tf_op jit(solution)/shard_map/ppermute | solution.py:217
  6.5 0.1 collective-permute-start.2
  6.6 1.3 reduce-window.6
  7.8 0.2 slice_reduce_fusion
  8.0 0.1 fusion.14
  8.1 0.1 broadcast_add_fusion
  8.2 0.8 pad_dynamic-slice_fusion
  9.0 0.1 fusion.13
  9.0 0.0 copy-start.4
  9.0 0.6 copy.58
  9.6 1.3 copy.71
  11.0 0.8 copy.59.seg_ref
  11.8 1.1 copy.70
  12.9 1.3 copy.60.cum_ref
  14.3 0.0 copy-done.5
  14.3 1.4 copy.61.beta_ref
  15.7 0.0 collective-permute-done
  15.7 0.0 copy-done.2
  15.7 1.1 pad_maximum_fusion
  16.8 0.0 copy-done.4
  16.8 28.7 %local_maps.1 = (bf16[8,256,128]{2,1,0:T(8,128)(2,1)}, f32[8,256,128]{2,1,0:T(8,128)}, bf16[16,192,128]{2,1,0:T(8,128)(2,1)}) custom-call(bf16[272,1024]{1,0:T(8,128)(2,1)} %get-tuple-element.19.q_ref.k_ref, bf16[272,1024]{1,0:T(8,128)(2,1)} %get-tuple-element.19.q_ref.k_ref, bf16[272,1024]{1,0:T(8,128)(2,1)} %get-tuple-element.20.v_ref, ...), custom_call_target="tpu_custom_call" | custom-call | tf_op jit(solution)/shard_map/local_maps/pallas_call | solution.py:129
  45.5 0.0 copy-start
  45.5 28.1 %all_to_all.15.maps_ref = bf16[16,192,128]{2,1,0:T(8,128)(2,1)} all-to-all(bf16[16,192,128]{2,1,0:T(8,128)(2,1)} %get-tuple-element.10), channel_id=1, replica_groups=mesh['group'=1,'ctx'=16,'head'=2] {'ctx'}, dimensions={0} | all-to-all | bytes 1572864 | tf_op jit(solution)/shard_map/all_to_all | solution.py:236
  73.6 3.6 %carried_states.1 = bf16[16,64,128]{2,1,0:T(8,128)(2,1)} custom-call(bf16[16,192,128]{2,1,0:T(8,128)(2,1)} %all_to_all.15.maps_ref), custom_call_target="tpu_custom_call" | custom-call | tf_op jit(solution)/shard_map/carried_states/pallas_call | solution.py:171
  77.2 3.5 %all-to-all-start.1 = ((bf16[16,64,128]{2,1,0:T(8,128)(2,1)}), bf16[16,64,128]{2,1,0:T(8,128)(2,1)S(1)}, u32[]{:S(2)}, u32[]{:S(2)}) async-start(bf16[16,64,128]{2,1,0:T(8,128)(2,1)} %carried_states.1), calls=%async_computation.1 | async-start | bytes 524288 | tf_op jit(solution)/shard_map/all_to_all | solution.py:237
  80.8 0.0 copy-done
  80.8 0.1 collective-permute-start.3
  80.9 9.1 %all-to-all-done.1 = bf16[16,64,128]{2,1,0:T(8,128)(2,1)S(1)} async-done(((bf16[16,64,128]{2,1,0:T(8,128)(2,1)}), bf16[16,64,128]{2,1,0:T(8,128)(2,1)S(1)}, u32[]{:S(2)}, u32[]{:S(2)}) %all-to-all-start.1) | async-done | bytes 262176 | tf_op jit(solution)/shard_map/all_to_all | solution.py:237
  90.0 0.0 copy-start.1
  90.0 0.7 copy-done.1
  90.7 0.0 copy-start.7
  90.7 0.0 copy-start.8
  90.7 0.0 copy-start.3
  90.7 6.1 %emitted_rows.1 = f32[256,2048]{1,0:T(8,128)} custom-call(bf16[8,256,128]{2,1,0:T(8,128)(2,1)} %get-tuple-element.8.qeff_ref, f32[8,256,128]{2,1,0:T(8,128)} %get-tuple-element.9.off_ref, bf16[8,128,128]{2,1,0:T(8,128)(2,1)} %bitcast.35, bf16[256,1024]{1,0:T(8,128)(2,1)} %gate_ref.1, f32[1,128]{1,0:T(1,128)} %bitcast.54, bf16[1024,2048]{1,0:T(8,128)(2,1)} %weight_ref.1), custom_call_target="tpu_custom_call" | custom-call | tf_op jit(solution)/shard_map/emitted_rows/pallas_call | solution.py:198
  96.8 0.0 copy-start.6
  96.8 2.1 dynamic-slice_convert_fusion
  98.9 0.0 collective-permute-start.1
  98.9 0.0 copy-done.7
  98.9 0.0 copy-done.8
  98.9 0.6 select_reduce_fusion
  99.5 3.7 %all-to-all-start.2 = ((f32[16,2,128]{2,1,0:T(2,128)}), f32[16,2,128]{2,1,0:T(2,128)S(1)}, u32[]{:S(2)}, u32[]{:S(2)}) async-start(f32[16,2,128]{2,1,0:T(2,128)} %bitcast.13), calls=%async_computation.2 | async-start | bytes 32768 | tf_op jit(solution)/shard_map/all_to_all | solution.py:484
  103.2 7.2 %all-to-all-done.2 = f32[16,2,128]{2,1,0:T(2,128)S(1)} async-done(((f32[16,2,128]{2,1,0:T(2,128)}), f32[16,2,128]{2,1,0:T(2,128)S(1)}, u32[]{:S(2)}, u32[]{:S(2)}) %all-to-all-start.2) | async-done | bytes 16416 | tf_op jit(solution)/shard_map/all_to_all | solution.py:484
  110.5 0.6 copy.68.weight_ref
  111.1 0.8 fusion.1.slot_ref
  111.9 0.0 collective-permute-done.1
  111.9 0.0 copy-done.3
  111.9 1.5 fusion.2
  113.5 0.0 copy-done.6
  113.5 1.0 fusion.4.x_ref
  114.5 0.0 collective-permute-done.3.down_other
  114.5 0.0 collective-permute-done.2.up_other
  114.5 160.9 %expert_sums.1 = f32[128,2048]{1,0:T(8,128)} custom-call(bf16[128,2048]{1,0:T(8,128)(2,1)} %fusion.4.x_ref, s32[4,2,512]{2,1,0:T(2,128)} %fusion.1.slot_ref, f32[4,2,512]{2,1,0:T(2,128)} %copy.68.weight_ref, bf16[1,2048,1024]{2,1,0:T(8,128)(2,1)} %up_mine.1, bf16[1,2048,1024]{2,1,0:T(8,128)(2,1)} %collective-permute-done.2.up_other, ...), custom_call_target="tpu_custom_call" | custom-call | tf_op jit(solution)/shard_map/expert_sums/pallas_call | solution.py:449
  275.4 2.1 fusion.5
  (11 shorter events, 0.2 us)
Async XLA Ops:
  0.0 15.7 %copy-start.2 = (bf16[256,1024]{1,0:T(8,128)(2,1)S(1)}, bf16[256,1024]{1,0:T(8,128)(2,1)}, u32[]{:S(2)}) copy-start(bf16[256,1024]{1,0:T(8,128)(2,1)} %param.17) | copy-start | bytes 1572868
  0.0 14.3 %copy-start.5 = (f32[256,8]{0,1:T(8,128)S(1)}, f32[256,8]{0,1:T(8,128)}, u32[]{:S(2)}) copy-start(f32[256,8]{0,1:T(8,128)} %param.19) | copy-start | bytes 24580
  1.6 14.0 %collective-permute-start = (bf16[16,2048]{1,0:T(8,128)(2,1)S(1)}, bf16[16,2048]{1,0:T(8,128)(2,1)S(1)}, u32[]{:S(2)}, u32[]{:S(2)}) collective-permute-start(bf16[16,2048]{1,0:T(8,128)(2,1)S(1)} %pad_maximum_fusion.2), channel_id=1, source_target_pairs={{0,2},{2,4},{4,6},{6,8},{8,10},{10,12},{12,14},{14,16},{16,18},{18... | collective-permute-start | bytes 196616 | tf_op jit(solution)/shard_map/ppermute | solution.py:217
  6.5 108.0 %collective-permute-start.2 = (bf16[1,2048,1024]{2,1,0:T(8,128)(2,1)}, bf16[1,2048,1024]{2,1,0:T(8,128)(2,1)}, u32[]{:S(2)}, u32[]{:S(2)}) collective-permute-start(bf16[1,2048,1024]{2,1,0:T(8,128)(2,1)} %up_mine.1), channel_id=1, source_target_pairs={{0,1},{1,0},{2,3},{3,2},{4,5},{5,4},{6,7},{7,6},{8,9},{9,8},{10,11... | collective-permute-start | bytes 12582920 | tf_op jit(solution)/shard_map/ppermute | solution.py:528
  9.0 7.7 %copy-start.4 = (s32[256]{0:T(256)}, s32[256]{0:T(256)S(1)}, u32[]{:S(2)}) copy-start(s32[256]{0:T(256)S(1)} %get-tuple-element.15) | copy-start | bytes 3076
  45.5 35.3 %copy-start = (bf16[1,512,2048]{2,1,0:T(8,128)(2,1)S(1)}, bf16[1,512,2048]{2,1,0:T(8,128)(2,1)}, u32[]{:S(2)}) copy-start(bf16[1,512,2048]{2,1,0:T(8,128)(2,1)} %down_mine.1) | copy-start | bytes 6291460
  77.2 12.8 %all-to-all-start.1 = ((bf16[16,64,128]{2,1,0:T(8,128)(2,1)}), bf16[16,64,128]{2,1,0:T(8,128)(2,1)S(1)}, u32[]{:S(2)}, u32[]{:S(2)}) async-start(bf16[16,64,128]{2,1,0:T(8,128)(2,1)} %carried_states.1), calls=%async_computation.1 | async-start | bytes 524288 | tf_op jit(solution)/shard_map/all_to_all | solution.py:237
  80.8 33.7 %collective-permute-start.3 = (bf16[1,512,2048]{2,1,0:T(8,128)(2,1)S(1)}, bf16[1,512,2048]{2,1,0:T(8,128)(2,1)}, u32[]{:S(2)}, u32[]{:S(2)}) collective-permute-start(bf16[1,512,2048]{2,1,0:T(8,128)(2,1)S(1)} %copy-done), channel_id=1, source_target_pairs={{0,1},{1,0},{2,3},{3,2},{4,5},{5,4},{6,7},{7,6},{8,9},{9,8},{10,11... | collective-permute-start | bytes 6291464 | tf_op jit(solution)/shard_map/ppermute | solution.py:529
  90.0 0.7 copy-start.1
  90.7 8.2 %copy-start.7 = (f32[128,10]{0,1:T(8,128)S(1)}, f32[128,10]{0,1:T(8,128)}, u32[]{:S(2)}) copy-start(f32[128,10]{0,1:T(8,128)} %param.29) | copy-start | bytes 15364
  90.7 8.2 %copy-start.8 = (s32[128,10]{0,1:T(8,128)S(1)}, s32[128,10]{0,1:T(8,128)}, u32[]{:S(2)}) copy-start(s32[128,10]{0,1:T(8,128)} %param.28) | copy-start | bytes 15364
  90.7 21.2 %copy-start.3 = (bf16[128,2048]{1,0:T(8,128)(2,1)S(1)}, bf16[128,2048]{1,0:T(8,128)(2,1)}, u32[]{:S(2)}) copy-start(bf16[128,2048]{1,0:T(8,128)(2,1)} %param.26) | copy-start | bytes 1572868
  96.8 16.7 %copy-start.6 = (f32[2048]{0:T(1024)S(1)}, f32[2048]{0:T(1024)}, u32[]{:S(2)}) copy-start(f32[2048]{0:T(1024)} %param.27) | copy-start | bytes 24580
  98.9 13.0 %collective-permute-start.1 = (bf16[128,2048]{1,0:T(8,128)(2,1)}, bf16[128,2048]{1,0:T(8,128)(2,1)S(1)}, u32[]{:S(2)}, u32[]{:S(2)}) collective-permute-start(bf16[128,2048]{1,0:T(8,128)(2,1)} %dynamic-slice_convert_fusion), channel_id=1, source_target_pairs={{0,1},{1,0},{2,3},{3,2},{4,5},{5,4},{6,7},{7,6},{8,9},{9,8},{10,11... | collective-permute-start | bytes 1572872 | tf_op jit(solution)/shard_map/ppermute | solution.py:539
  99.5 10.9 %all-to-all-start.2 = ((f32[16,2,128]{2,1,0:T(2,128)}), f32[16,2,128]{2,1,0:T(2,128)S(1)}, u32[]{:S(2)}, u32[]{:S(2)}) async-start(f32[16,2,128]{2,1,0:T(2,128)} %bitcast.13), calls=%async_computation.2 | async-start | bytes 32768 | tf_op jit(solution)/shard_map/all_to_all | solution.py:484

commit v3 on v2

--- a/solution.py
+++ b/solution.py
@@ -69,9 +69,10 @@
 
 def local_kernel(
     q_ref, k_ref, v_ref, qt_ref, kt_ref, vt_ref, seg_ref, segrow_ref,
-    cum_ref, cumrow_ref, beta_ref, qeff_ref, off_ref, maps_ref,
+    cum_ref, cumrow_ref, beta_ref, table_ref, qeff_ref, off_ref, maps_ref,
 ):
     rows = qeff_ref.shape[1]
+    maps_ref[:, DK + DV // 2 :, :] = table_ref[...]
     seg = seg_ref[...]
     match = [None] + [(seg[:, lag : lag + 1] == seg[:, 0:1]).astype(jnp.float32) for lag in range(1, 4)]
     ids = seg[:, 0:1]
@@ -116,13 +117,14 @@
         for half in range(2):
             at = member * 2 + half
             maps_ref[at, :DK, :] = forward.astype(jnp.bfloat16)
-            maps_ref[at, DK:, :] = shift_t[half * (DV // 2) : (half + 1) * (DV // 2)].astype(jnp.bfloat16)
-
-
-def local_maps(pair, value, pair_taps, value_taps, seg, segrow, cum, cumrow, beta):
+            maps_ref[at, DK : DK + DV // 2, :] = shift_t[half * (DV // 2) : (half + 1) * (DV // 2)].astype(jnp.bfloat16)
+
+
+def local_maps(pair, value, pair_taps, value_taps, seg, segrow, cum, cumrow, beta, table):
     heads, rows = beta.shape[:2]
     key_heads = pair.shape[1] // (2 * DK)
     per = heads // key_heads
+    extra = table.shape[1]
     padded = pair.shape[0]
     taps = pair_taps.shape[0]
     whole = lambda g: (0, 0)
@@ -141,20 +143,21 @@
             pl.BlockSpec((per, rows, 1), lambda g: (g, 0, 0)),
             pl.BlockSpec((per, 1, rows), lambda g: (g, 0, 0)),
             pl.BlockSpec((per, rows, 1), lambda g: (g, 0, 0)),
+            pl.BlockSpec((2 * per, extra, DK), lambda g: (g, 0, 0)),
         ],
         out_specs=[
             pl.BlockSpec((per, rows, DK), lambda g: (g, 0, 0)),
             pl.BlockSpec((per, rows, DV), lambda g: (g, 0, 0)),
-            pl.BlockSpec((2 * per, DK + DV // 2, DK), lambda g: (g, 0, 0)),
+            pl.BlockSpec((2 * per, DK + DV // 2 + extra, DK), lambda g: (g, 0, 0)),
         ],
         out_shape=[
             jax.ShapeDtypeStruct((heads, rows, DK), jnp.bfloat16),
             jax.ShapeDtypeStruct((heads, rows, DV), jnp.float32),
-            jax.ShapeDtypeStruct((2 * heads, DK + DV // 2, DK), jnp.bfloat16),
+            jax.ShapeDtypeStruct((2 * heads, DK + DV // 2 + extra, DK), jnp.bfloat16),
         ],
         compiler_params=pltpu.CompilerParams(vmem_limit_bytes=VMEM_MOST),
         name="local_maps",
-    )(pair, pair, value, pair_taps, pair_taps, value_taps, seg, segrow, cum, cumrow, beta)
+    )(pair, pair, value, pair_taps, pair_taps, value_taps, seg, segrow, cum, cumrow, beta, table)
 
 
 def carry_kernel(maps_ref, states_ref):
@@ -163,7 +166,7 @@
         states_ref[at] = state.astype(jnp.bfloat16)
         if at + 1 < maps_ref.shape[0]:
             moved = dot16(state, maps_ref[at, :DK, :], NT)
-            state = moved + maps_ref[at, DK:, :].astype(jnp.float32)
+            state = moved + maps_ref[at, DK : DK + DV // 2, :].astype(jnp.float32)
 
 
 def carried_states(maps):
@@ -206,7 +209,7 @@
 
 def mixer(
     pair_raw, value_raw, gate_raw, write_strength, log_decay, segment_ids,
-    pair_filter, value_filter, norm_gain, out_weight,
+    pair_filter, value_filter, norm_gain, out_weight, table,
 ):
     rows = pair_raw.shape[0]
     taps = value_filter.shape[0]
@@ -231,12 +234,14 @@
         cum[:, :, None],
         cum[:, None, :],
         write_strength.T[:, :, None],
+        table,
     )
     heads = qeff.shape[0]
     arrived = lax.all_to_all(maps, "ctx", split_axis=0, concat_axis=0, tiled=True)
     states = lax.all_to_all(carried_states(arrived), "ctx", split_axis=0, concat_axis=0, tiled=True)
     states = states.reshape(heads, DV, DK)
-    return emitted_rows(qeff, off, states, gate_raw, norm_gain[None, :], out_weight)
+    partial = emitted_rows(qeff, off, states, gate_raw, norm_gain[None, :], out_weight)
+    return partial, arrived[:, DK + DV // 2 :]
 
 PLANE = 4
 AGZ, AGX, AGY, AGA, AGB, DA, DB, XA, XB, YA, YB, RSZ = range(12)
@@ -309,9 +314,25 @@
         copy(AGX, k, got.at[own], got.at[own], beside_x).start()
         copy(AGY, k, got.at[own], got.at[own], beside_y).start()
 
+    def share_along_z(k):
+        copy(AGZ, k, got.at[me], got.at[me], along_z(k)).start()
+
+    def pass_on(k):
+        across_x, across_y = block(k, False, True), block(k, True, False)
+        arrived(AGX, k, got.at[across_x], beside_x)
+        copy(AGA, k, got.at[across_x, first], got.at[across_x, first], beside_y).start()
+        arrived(AGY, k, got.at[across_y], beside_y)
+        copy(AGB, k, got.at[across_y, second], got.at[across_y, second], beside_x).start()
+
+    def take_from_z(k):
+        arrived(AGZ, k, got.at[along_z(k)], along_z(k))
+        share_in_plane(k)
+
     share_in_plane(0)
-    for k in range(1, planes):
-        copy(AGZ, k, got.at[me], got.at[me], along_z(k)).start()
+    share_along_z(1)
+    pass_on(0)
+    share_along_z(2)
+    take_from_z(1)
     for load in loads:
         load.wait()
 
@@ -382,16 +403,14 @@
         copy(RSZ, k, sums.at[k], from_z.at[k], along_z(k)).start()
 
     def turn(k, unused):
-        across_x, across_y = block(k, False, True), block(k, True, False)
-        arrived(AGX, k, got.at[across_x], beside_x)
-        copy(AGA, k, got.at[across_x, first], got.at[across_x, first], beside_y).start()
-        arrived(AGY, k, got.at[across_y], beside_y)
-        copy(AGB, k, got.at[across_y, second], got.at[across_y, second], beside_x).start()
-
         @pl.when(k < planes - 1)
         def _():
-            arrived(AGZ, k + 1, got.at[along_z(k + 1)], along_z(k + 1))
-            share_in_plane(k + 1)
+            pass_on(k + 1)
+
+        @pl.when(k == 0)
+        def _():
+            share_along_z(3)
+            take_from_z(2)
 
         across = block(k, True, True)
         arrived(AGA, k, got.at[across, first], beside_y)
@@ -401,6 +420,10 @@
         @pl.when(k >= 1)
         def _():
             give_first(k)
+
+        @pl.when(k == 1)
+        def _():
+            take_from_z(3)
 
         @pl.when(k >= 2)
         def _():
@@ -475,15 +498,19 @@
     )(x, slot, weight, up_mine, up_other, down_mine, down_other)
 
 
-def route_tables(routes, route_weights):
+def weights_by_chip(routes, route_weights):
     peers, cores = lax.axis_size("ctx"), lax.axis_size("head")
     experts = jnp.arange(peers * cores, dtype=jnp.int32)
     named = (routes[None] == experts[:, None, None]).astype(jnp.float32)
-    dense = jnp.sum(named * route_weights[None], axis=2)
-    tokens = routes.shape[0]
-    seen = lax.all_to_all(
-        dense.reshape(peers, cores, tokens), "ctx", split_axis=0, concat_axis=0, tiled=True
-    )
+    dense = jnp.sum(named * route_weights[None], axis=2).astype(jnp.bfloat16)
+    dense = dense.reshape(peers, cores, routes.shape[0])
+    return jnp.pad(dense, ((0, 0), (0, 16 - cores), (0, 0)))
+
+
+def route_tables(seen):
+    peers, cores = lax.axis_size("ctx"), lax.axis_size("head")
+    tokens = seen.shape[2]
+    seen = seen[:, :cores].astype(jnp.float32)
     seen = jnp.where(lax.axis_index("head") == 0, seen, seen[:, ::-1])
     seen = seen.reshape(peers // PLANE, PLANE, cores, tokens).swapaxes(1, 2)
     seen = seen.reshape(peers // PLANE, cores, PLANE * tokens)
@@ -527,11 +554,12 @@
     devices_all = lax.axis_size("ctx") * lax.axis_size("head")
     up_other = lax.ppermute(expert_up, "head", swap)
     down_other = lax.ppermute(expert_down, "head", swap)
-    slot, weight = route_tables(routes, route_weights)
-    partial = mixer(
+    partial, seen = mixer(
         pair_raw, value_raw, gate_raw, write_strength, log_decay, segment_ids,
         pair_filter, value_filter, norm_gain, out_weight,
+        weights_by_chip(routes, route_weights),
     )
+    slot, weight = route_tables(seen)
     half = partial.shape[0] // 2
     core = lax.axis_index("head")
     mine = lax.dynamic_slice_in_dim(partial, core * half, half)

time: 283 us -> 275 us (0.972)
  waiting for transfers between devices: 16.3 us -> 8.84 us
  starting transfers between devices: 12.2 us -> 8.71 us
    all_to_all x1 -> x0, waiting for transfers between devices: 7.19 us -> none  [route_tables(): lax.all_to_all(dense.reshape(peers, cores, tokens), 'ctx', split_axis=0,...]
    all_to_all x1 -> x0, starting transfers between devices: 3.68 us -> none  [route_tables(): lax.all_to_all(dense.reshape(peers, cores, tokens), 'ctx', split_axis=0,...]
  transfers between devices with their start and end apart: 6 -> 5, of which waited for: 2 -> 1; matrix products, arithmetic and copies ran while one was open for 6% -> 7% of each run, Pallas kernels for 14% -> 14%
where the time goes in v3:
time: 275 us; the launch traced here: 271 us
  Pallas kernels  201 us (73%)
  blocking collectives  29.4 us (11%)
  local copies, waits for them, and re-layouts  12.8 us (5%)
  waiting for transfers between devices  8.84 us (3%)
  other arithmetic  8.76 us (3%)
  starting transfers between devices  8.71 us (3%)
    pallas_call x1, Pallas kernels, expert_sums(): pl.pallas_call(expert_kernel, out_shape=jax.ShapeDtypeStruct((tokens, wid...  163 us
    all_to_all x1, blocking collectives, mixer(): lax.all_to_all(maps, 'ctx', split_axis=0, concat_axis=0, tiled=True)  29.4 us
    pallas_call x1, Pallas kernels, local_maps(): pl.pallas_call(local_kernel, grid=(key_heads,), in_specs=[pl.BlockSpec((p...  28.8 us
    all_to_all x1, waiting for transfers between devices, mixer(): lax.all_to_all(carried_states(arrived), 'ctx', split_axis=0, concat_axis=...  8.83 us
    pallas_call x1, Pallas kernels, emitted_rows(): pl.pallas_call(emit_kernel, out_shape=jax.ShapeDtypeStruct((rows, weight....  6.1 us
  transfers between devices with their start and end apart: 5, of which 1 were waited for; matrix products, arithmetic and copies ran while one was open for 7% of the time, Pallas kernels for 14%

profile of v3, /device:TPU:0, one launch (start us, length us, event | category | flops | bytes accessed | tf_op | source)
XLA Modules:
  0.0 270.8 jit_solution(10401150114367294625)
XLA Ops:
  0.0 0.0 copy-start.2
  0.0 0.0 copy-start.6
  0.0 0.0 copy-start.8
  0.0 0.0 copy-start.9
  0.0 0.8 slice.39
  0.9 0.8 slice.41
  1.6 4.9 %collective-permute-start = (bf16[16,2048]{1,0:T(8,128)(2,1)S(1)}, bf16[16,2048]{1,0:T(8,128)(2,1)S(1)}, u32[]{:S(2)}, u32[]{:S(2)}) collective-permute-start(bf16[16,2048]{1,0:T(8,128)(2,1)S(1)} %pad_maximum_fusion.2), channel_id=1, source_target_pairs={{0,2},{2,4},{4,6},{6,8},{8,10},{10,12},{12,14},{14,16},{16,18},{18... | collective-permute-start | bytes 196616 | tf_op jit(solution)/shard_map/ppermute | solution.py:220
  6.5 0.1 collective-permute-start.2
  6.6 1.3 reduce-window.6
  7.8 0.2 slice_reduce_fusion
  8.0 0.1 fusion.13
  8.1 0.1 broadcast_add_fusion
  8.2 0.8 pad_dynamic-slice_fusion
  9.0 0.1 fusion.12
  9.0 0.0 copy-start.5
  9.0 0.6 copy.45
  9.6 1.3 copy.56
  11.0 0.8 copy.46.seg_ref
  11.8 1.1 copy.55
  12.9 1.4 copy.47.cum_ref
  14.3 0.0 copy-done.6
  14.3 1.4 copy.48.beta_ref
  15.6 0.0 copy-done.8
  15.6 0.0 copy-done.9
  15.7 0.6 pad.5.table_ref
  16.3 0.0 collective-permute-done
  16.3 0.0 copy-done.2
  16.3 1.1 pad_maximum_fusion
  17.4 0.0 copy-done.5
  17.4 28.8 %local_maps.1 = (bf16[8,256,128]{2,1,0:T(8,128)(2,1)}, f32[8,256,128]{2,1,0:T(8,128)}, bf16[16,208,128]{2,1,0:T(8,128)(2,1)}) custom-call(bf16[272,1024]{1,0:T(8,128)(2,1)} %get-tuple-element.19.q_ref.k_ref, bf16[272,1024]{1,0:T(8,128)(2,1)} %get-tuple-element.19.q_ref.k_ref, bf16[272,1024]{1,0:T(8,128)(2,1)} %get-tuple-element.20.v_ref, ...), custom_call_target="tpu_custom_call" | custom-call | tf_op jit(solution)/shard_map/local_maps/pallas_call | solution.py:131
  46.2 0.0 copy-start
  46.2 29.4 %all_to_all.10.maps_ref = bf16[16,208,128]{2,1,0:T(8,128)(2,1)} all-to-all(bf16[16,208,128]{2,1,0:T(8,128)(2,1)} %get-tuple-element.10), channel_id=1, replica_groups=mesh['group'=1,'ctx'=16,'head'=2] {'ctx'}, dimensions={0} | all-to-all | bytes 1703936 | tf_op jit(solution)/shard_map/all_to_all | solution.py:240
  75.6 3.6 %carried_states.1 = bf16[16,64,128]{2,1,0:T(8,128)(2,1)} custom-call(bf16[16,208,128]{2,1,0:T(8,128)(2,1)} %all_to_all.10.maps_ref), custom_call_target="tpu_custom_call" | custom-call | tf_op jit(solution)/shard_map/carried_states/pallas_call | solution.py:174
  79.2 3.7 %all-to-all-start.1 = ((bf16[16,64,128]{2,1,0:T(8,128)(2,1)}), bf16[16,64,128]{2,1,0:T(8,128)(2,1)S(1)}, u32[]{:S(2)}, u32[]{:S(2)}) async-start(bf16[16,64,128]{2,1,0:T(8,128)(2,1)} %carried_states.1), calls=%async_computation.1 | async-start | bytes 524288 | tf_op jit(solution)/shard_map/all_to_all | solution.py:241
  82.9 0.0 copy-done
  83.0 0.1 collective-permute-start.3
  83.0 8.8 %all-to-all-done.1 = bf16[16,64,128]{2,1,0:T(8,128)(2,1)S(1)} async-done(((bf16[16,64,128]{2,1,0:T(8,128)(2,1)}), bf16[16,64,128]{2,1,0:T(8,128)(2,1)S(1)}, u32[]{:S(2)}, u32[]{:S(2)}) %all-to-all-start.1) | async-done | bytes 262176 | tf_op jit(solution)/shard_map/all_to_all | solution.py:241
  91.9 0.0 copy-start.1
  91.9 0.7 copy-done.1
  92.6 0.0 copy-start.3
  92.6 6.1 %emitted_rows.1 = f32[256,2048]{1,0:T(8,128)} custom-call(bf16[8,256,128]{2,1,0:T(8,128)(2,1)} %get-tuple-element.8.qeff_ref, f32[8,256,128]{2,1,0:T(8,128)} %get-tuple-element.9.off_ref, bf16[8,128,128]{2,1,0:T(8,128)(2,1)} %bitcast.31, bf16[256,1024]{1,0:T(8,128)(2,1)} %gate_ref.1, f32[1,128]{1,0:T(1,128)} %bitcast.49, bf16[1024,2048]{1,0:T(8,128)(2,1)} %weight_ref.1), custom_call_target="tpu_custom_call" | custom-call | tf_op jit(solution)/shard_map/emitted_rows/pallas_call | solution.py:201
  98.7 0.0 copy-start.7
  98.7 2.1 dynamic-slice_convert_fusion
  100.8 0.0 collective-permute-start.1
  100.8 0.8 slice_convert_fusion
  101.6 0.8 broadcast_select_fusion
  102.4 0.0 copy-start.4
  102.4 0.8 fusion.1.slot_ref
  103.2 0.0 collective-permute-done.1
  103.2 0.0 copy-done.3
  103.2 1.5 fusion.2
  104.8 0.0 copy-done.7
  104.8 1.0 fusion.4.x_ref
  105.8 0.0 collective-permute-done.3.down_other
  105.8 0.0 collective-permute-done.2.up_other
  105.8 0.0 copy-done.4
  105.8 162.9 %expert_sums.1 = f32[128,2048]{1,0:T(8,128)} custom-call(bf16[128,2048]{1,0:T(8,128)(2,1)} %fusion.4.x_ref, s32[4,2,512]{2,1,0:T(2,128)} %fusion.1.slot_ref, f32[4,2,512]{2,1,0:T(2,128)} %copy-done.4, bf16[1,2048,1024]{2,1,0:T(8,128)(2,1)} %up_mine.1, bf16[1,2048,1024]{2,1,0:T(8,128)(2,1)} %collective-permute-done.2.up_other, ...), custom_call_target="tpu_custom_call" | custom-call | tf_op jit(solution)/shard_map/expert_sums/pallas_call | solution.py:472
  268.7 2.1 fusion.5
  (11 shorter events, 0.2 us)
Async XLA Ops:
  0.0 16.3 %copy-start.2 = (bf16[256,1024]{1,0:T(8,128)(2,1)S(1)}, bf16[256,1024]{1,0:T(8,128)(2,1)}, u32[]{:S(2)}) copy-start(bf16[256,1024]{1,0:T(8,128)(2,1)} %param.17) | copy-start | bytes 1572868
  0.0 14.3 %copy-start.6 = (f32[256,8]{0,1:T(8,128)S(1)}, f32[256,8]{0,1:T(8,128)}, u32[]{:S(2)}) copy-start(f32[256,8]{0,1:T(8,128)} %param.19) | copy-start | bytes 24580
  0.0 15.6 %copy-start.8 = (f32[128,10]{0,1:T(8,128)S(1)}, f32[128,10]{0,1:T(8,128)}, u32[]{:S(2)}) copy-start(f32[128,10]{0,1:T(8,128)} %param.29) | copy-start | bytes 15364
  0.0 15.6 %copy-start.9 = (s32[128,10]{0,1:T(8,128)S(1)}, s32[128,10]{0,1:T(8,128)}, u32[]{:S(2)}) copy-start(s32[128,10]{0,1:T(8,128)} %param.28) | copy-start | bytes 15364
  1.6 14.7 %collective-permute-start = (bf16[16,2048]{1,0:T(8,128)(2,1)S(1)}, bf16[16,2048]{1,0:T(8,128)(2,1)S(1)}, u32[]{:S(2)}, u32[]{:S(2)}) collective-permute-start(bf16[16,2048]{1,0:T(8,128)(2,1)S(1)} %pad_maximum_fusion.2), channel_id=1, source_target_pairs={{0,2},{2,4},{4,6},{6,8},{8,10},{10,12},{12,14},{14,16},{16,18},{18... | collective-permute-start | bytes 196616 | tf_op jit(solution)/shard_map/ppermute | solution.py:220
  6.5 99.3 %collective-permute-start.2 = (bf16[1,2048,1024]{2,1,0:T(8,128)(2,1)}, bf16[1,2048,1024]{2,1,0:T(8,128)(2,1)}, u32[]{:S(2)}, u32[]{:S(2)}) collective-permute-start(bf16[1,2048,1024]{2,1,0:T(8,128)(2,1)} %up_mine.1), channel_id=1, source_target_pairs={{0,1},{1,0},{2,3},{3,2},{4,5},{5,4},{6,7},{7,6},{8,9},{9,8},{10,11... | collective-permute-start | bytes 12582920 | tf_op jit(solution)/shard_map/ppermute | solution.py:555
  9.0 8.4 %copy-start.5 = (s32[256]{0:T(256)}, s32[256]{0:T(256)S(1)}, u32[]{:S(2)}) copy-start(s32[256]{0:T(256)S(1)} %get-tuple-element.15) | copy-start | bytes 3076
  46.2 36.8 %copy-start = (bf16[1,512,2048]{2,1,0:T(8,128)(2,1)S(1)}, bf16[1,512,2048]{2,1,0:T(8,128)(2,1)}, u32[]{:S(2)}) copy-start(bf16[1,512,2048]{2,1,0:T(8,128)(2,1)} %down_mine.1) | copy-start | bytes 6291460
  79.2 12.6 %all-to-all-start.1 = ((bf16[16,64,128]{2,1,0:T(8,128)(2,1)}), bf16[16,64,128]{2,1,0:T(8,128)(2,1)S(1)}, u32[]{:S(2)}, u32[]{:S(2)}) async-start(bf16[16,64,128]{2,1,0:T(8,128)(2,1)} %carried_states.1), calls=%async_computation.1 | async-start | bytes 524288 | tf_op jit(solution)/shard_map/all_to_all | solution.py:241
  83.0 22.8 %collective-permute-start.3 = (bf16[1,512,2048]{2,1,0:T(8,128)(2,1)S(1)}, bf16[1,512,2048]{2,1,0:T(8,128)(2,1)}, u32[]{:S(2)}, u32[]{:S(2)}) collective-permute-start(bf16[1,512,2048]{2,1,0:T(8,128)(2,1)S(1)} %copy-done), channel_id=1, source_target_pairs={{0,1},{1,0},{2,3},{3,2},{4,5},{5,4},{6,7},{7,6},{8,9},{9,8},{10,11... | collective-permute-start | bytes 6291464 | tf_op jit(solution)/shard_map/ppermute | solution.py:556
  91.9 0.7 copy-start.1
  92.6 10.6 %copy-start.3 = (bf16[128,2048]{1,0:T(8,128)(2,1)S(1)}, bf16[128,2048]{1,0:T(8,128)(2,1)}, u32[]{:S(2)}) copy-start(bf16[128,2048]{1,0:T(8,128)(2,1)} %param.26) | copy-start | bytes 1572868
  98.7 6.1 %copy-start.7 = (f32[2048]{0:T(1024)S(1)}, f32[2048]{0:T(1024)}, u32[]{:S(2)}) copy-start(f32[2048]{0:T(1024)} %param.27) | copy-start | bytes 24580
  100.8 2.4 collective-permute-start.1
  102.4 3.4 %copy-start.4 = (f32[4,2,512]{2,1,0:T(2,128)}, f32[4,2,512]{2,1,0:T(2,128)S(1)}, u32[]{:S(2)}) copy-start(f32[4,2,512]{2,1,0:T(2,128)S(1)} %reshape.89.weight_ref) | copy-start | bytes 49156

commit v4 on v3

--- a/solution.py
+++ b/solution.py
@@ -55,16 +55,20 @@
     return x * lax.rsqrt(jnp.sum(x * x, axis=-1, keepdims=True) + EPS)
 
 
-def inverse_unit_lower(coupling, row, col):
-    size = coupling.shape[0]
+def inverses_unit_lower(couplings, row, col):
+    size = couplings[0].shape[0]
     apart = row ^ col
-    inverse = jnp.where(row == col, 1.0, 0.0) - jnp.where(apart == 1, coupling, 0.0)
+    eye = jnp.where(row == col, 1.0, 0.0)
+    found = [eye - jnp.where(apart == 1, c, 0.0) for c in couplings]
     step = 2
     while step < size:
-        cross = jnp.where((apart >= step) & (apart < 2 * step), coupling, 0.0)
-        inverse = inverse - dot16(inverse, dot16(cross, inverse))
+        band = (apart >= step) & (apart < 2 * step)
+        crosses = [jnp.where(band, c, 0.0) for c in couplings]
+        found16 = [f.astype(jnp.bfloat16) for f in found]
+        inner = [dot16(c, f) for c, f in zip(crosses, found16)]
+        found = [f - dot16(f16, i) for f, f16, i in zip(found, found16, inner)]
         step *= 2
-    return inverse
+    return found
 
 
 def local_kernel(
@@ -94,18 +98,27 @@
     eye = (
         lax.broadcasted_iota(jnp.int32, (DK, DK), 0) == lax.broadcasted_iota(jnp.int32, (DK, DK), 1)
     ).astype(jnp.float32)
-    for member in range(qeff_ref.shape[0]):
+    decays = [
+        jnp.exp(jnp.where(causal, cum_ref[member] - cumrow_ref[member], 0.0))
+        for member in range(qeff_ref.shape[0])
+    ]
+    found = inverses_unit_lower(
+        [
+            jnp.where(strictly, gram * decay * beta_ref[member], 0.0)
+            for member, decay in enumerate(decays)
+        ],
+        row,
+        col,
+    )
+    for member, decay in enumerate(decays):
         lanes = slice(member * DV, (member + 1) * DV)
         values = filtered(v_ref, vt_ref, match, lanes)
         cum = cum_ref[member]
         beta = beta_ref[member]
-        decay = jnp.exp(jnp.where(causal, cum - cumrow_ref[member], 0.0))
-        coupling = jnp.where(strictly, gram * decay * beta, 0.0)
         within = jnp.where(causal, cross * decay, 0.0)
         grown = jnp.exp(cum) * carried
-        inverse = inverse_unit_lower(coupling, row, col)
         stacked = jnp.concatenate([values * beta, k32 * (beta * grown)], axis=1)
-        solved = dot16(inverse, stacked)
+        solved = dot16(found[member], stacked)
         both = dot16(within, solved)
         off_ref[member] = both[:, :DV]
         qeff_ref[member] = (q32 * grown - both[:, DV:]).astype(jnp.bfloat16)

time: 275 us -> 265 us (0.964)
  Pallas kernels: 201 us -> 191 us
    pallas_call x1, Pallas kernels: 28.8 us -> 18.7 us  [local_maps(): pl.pallas_call(local_kernel, grid=(key_heads,), in_specs=[pl.BlockSpec((p...]
  transfers between devices with their start and end apart: 5 -> 5, of which waited for: 1 -> 1; matrix products, arithmetic and copies ran while one was open for 7% -> 7% of each run, Pallas kernels for 14% -> 11%
where the time goes in v4:
time: 265 us; the launch traced here: 261 us
  Pallas kernels  191 us (72%)
  blocking collectives  29.4 us (11%)
  local copies, waits for them, and re-layouts  12.8 us (5%)
  waiting for transfers between devices  8.84 us (3%)
  other arithmetic  8.76 us (3%)
  starting transfers between devices  8.71 us (3%)
    pallas_call x1, Pallas kernels, expert_sums(): pl.pallas_call(expert_kernel, out_shape=jax.ShapeDtypeStruct((tokens, wid...  163 us
    all_to_all x1, blocking collectives, mixer(): lax.all_to_all(maps, 'ctx', split_axis=0, concat_axis=0, tiled=True)  29.4 us
    pallas_call x1, Pallas kernels, local_maps(): pl.pallas_call(local_kernel, grid=(key_heads,), in_specs=[pl.BlockSpec((p...  18.7 us
    all_to_all x1, waiting for transfers between devices, mixer(): lax.all_to_all(carried_states(arrived), 'ctx', split_axis=0, concat_axis=...  8.83 us
    pallas_call x1, Pallas kernels, emitted_rows(): pl.pallas_call(emit_kernel, out_shape=jax.ShapeDtypeStruct((rows, weight....  6.1 us
  transfers between devices with their start and end apart: 5, of which 1 were waited for; matrix products, arithmetic and copies ran while one was open for 7% of the time, Pallas kernels for 11%

profile of v4, /device:TPU:0, one launch (start us, length us, event | category | flops | bytes accessed | tf_op | source)
XLA Modules:
  0.0 260.7 jit_solution(10737654987944688916)
XLA Ops:
  0.0 0.0 copy-start.2
  0.0 0.0 copy-start.6
  0.0 0.0 copy-start.8
  0.0 0.0 copy-start.9
  0.0 0.8 slice.39
  0.9 0.8 slice.41
  1.6 4.9 %collective-permute-start = (bf16[16,2048]{1,0:T(8,128)(2,1)S(1)}, bf16[16,2048]{1,0:T(8,128)(2,1)S(1)}, u32[]{:S(2)}, u32[]{:S(2)}) collective-permute-start(bf16[16,2048]{1,0:T(8,128)(2,1)S(1)} %pad_maximum_fusion.2), channel_id=1, source_target_pairs={{0,2},{2,4},{4,6},{6,8},{8,10},{10,12},{12,14},{14,16},{16,18},{18... | collective-permute-start | bytes 196616 | tf_op jit(solution)/shard_map/ppermute | solution.py:233
  6.5 0.1 collective-permute-start.2
  6.6 1.3 reduce-window.6
  7.8 0.2 slice_reduce_fusion
  8.0 0.1 fusion.13
  8.1 0.1 broadcast_add_fusion
  8.2 0.8 pad_dynamic-slice_fusion
  9.0 0.1 fusion.12
  9.0 0.0 copy-start.5
  9.0 0.6 copy.45
  9.6 1.3 copy.56
  11.0 0.8 copy.46.seg_ref
  11.8 1.1 copy.55
  12.9 1.4 copy.47.cum_ref
  14.3 0.0 copy-done.6
  14.3 1.4 copy.48.beta_ref
  15.6 0.0 copy-done.8
  15.6 0.0 copy-done.9
  15.7 0.6 pad.5.table_ref
  16.3 0.0 collective-permute-done
  16.3 0.0 copy-done.2
  16.3 1.1 pad_maximum_fusion
  17.4 0.0 copy-done.5
  17.4 18.7 %local_maps.1 = (bf16[8,256,128]{2,1,0:T(8,128)(2,1)}, f32[8,256,128]{2,1,0:T(8,128)}, bf16[16,208,128]{2,1,0:T(8,128)(2,1)}) custom-call(bf16[272,1024]{1,0:T(8,128)(2,1)} %get-tuple-element.19.q_ref.k_ref, bf16[272,1024]{1,0:T(8,128)(2,1)} %get-tuple-element.19.q_ref.k_ref, bf16[272,1024]{1,0:T(8,128)(2,1)} %get-tuple-element.20.v_ref, ...), custom_call_target="tpu_custom_call" | custom-call | tf_op jit(solution)/shard_map/local_maps/pallas_call | solution.py:144
  36.1 0.0 copy-start
  36.1 29.4 %all_to_all.10.maps_ref = bf16[16,208,128]{2,1,0:T(8,128)(2,1)} all-to-all(bf16[16,208,128]{2,1,0:T(8,128)(2,1)} %get-tuple-element.10), channel_id=1, replica_groups=mesh['group'=1,'ctx'=16,'head'=2] {'ctx'}, dimensions={0} | all-to-all | bytes 1703936 | tf_op jit(solution)/shard_map/all_to_all | solution.py:253
  65.5 3.6 %carried_states.1 = bf16[16,64,128]{2,1,0:T(8,128)(2,1)} custom-call(bf16[16,208,128]{2,1,0:T(8,128)(2,1)} %all_to_all.10.maps_ref), custom_call_target="tpu_custom_call" | custom-call | tf_op jit(solution)/shard_map/carried_states/pallas_call | solution.py:187
  69.1 3.7 %all-to-all-start.1 = ((bf16[16,64,128]{2,1,0:T(8,128)(2,1)}), bf16[16,64,128]{2,1,0:T(8,128)(2,1)S(1)}, u32[]{:S(2)}, u32[]{:S(2)}) async-start(bf16[16,64,128]{2,1,0:T(8,128)(2,1)} %carried_states.1), calls=%async_computation.1 | async-start | bytes 524288 | tf_op jit(solution)/shard_map/all_to_all | solution.py:254
  72.9 0.0 copy-done
  72.9 0.1 collective-permute-start.3
  73.0 8.8 %all-to-all-done.1 = bf16[16,64,128]{2,1,0:T(8,128)(2,1)S(1)} async-done(((bf16[16,64,128]{2,1,0:T(8,128)(2,1)}), bf16[16,64,128]{2,1,0:T(8,128)(2,1)S(1)}, u32[]{:S(2)}, u32[]{:S(2)}) %all-to-all-start.1) | async-done | bytes 262176 | tf_op jit(solution)/shard_map/all_to_all | solution.py:254
  81.8 0.0 copy-start.1
  81.8 0.7 copy-done.1
  82.5 0.0 copy-start.3
  82.5 6.1 %emitted_rows.1 = f32[256,2048]{1,0:T(8,128)} custom-call(bf16[8,256,128]{2,1,0:T(8,128)(2,1)} %get-tuple-element.8.qeff_ref, f32[8,256,128]{2,1,0:T(8,128)} %get-tuple-element.9.off_ref, bf16[8,128,128]{2,1,0:T(8,128)(2,1)} %bitcast.31, bf16[256,1024]{1,0:T(8,128)(2,1)} %gate_ref.1, f32[1,128]{1,0:T(1,128)} %bitcast.49, bf16[1024,2048]{1,0:T(8,128)(2,1)} %weight_ref.1), custom_call_target="tpu_custom_call" | custom-call | tf_op jit(solution)/shard_map/emitted_rows/pallas_call | solution.py:214
  88.6 0.0 copy-start.7
  88.6 2.1 dynamic-slice_convert_fusion
  90.7 0.0 collective-permute-start.1
  90.7 0.8 slice_convert_fusion
  91.5 0.8 broadcast_select_fusion
  92.3 0.0 copy-start.4
  92.3 0.8 fusion.1.slot_ref
  93.1 0.0 collective-permute-done.1
  93.1 0.0 copy-done.3
  93.1 1.5 fusion.2
  94.7 0.0 copy-done.7
  94.7 1.0 fusion.4.x_ref
  95.7 0.0 collective-permute-done.3.down_other
  95.7 0.0 collective-permute-done.2.up_other
  95.7 0.0 copy-done.4
  95.7 162.8 %expert_sums.1 = f32[128,2048]{1,0:T(8,128)} custom-call(bf16[128,2048]{1,0:T(8,128)(2,1)} %fusion.4.x_ref, s32[4,2,512]{2,1,0:T(2,128)} %fusion.1.slot_ref, f32[4,2,512]{2,1,0:T(2,128)} %copy-done.4, bf16[1,2048,1024]{2,1,0:T(8,128)(2,1)} %up_mine.1, bf16[1,2048,1024]{2,1,0:T(8,128)(2,1)} %collective-permute-done.2.up_other, ...), custom_call_target="tpu_custom_call" | custom-call | tf_op jit(solution)/shard_map/expert_sums/pallas_call | solution.py:485
  258.6 2.1 fusion.5
  (11 shorter events, 0.2 us)
Async XLA Ops:
  0.0 16.3 %copy-start.2 = (bf16[256,1024]{1,0:T(8,128)(2,1)S(1)}, bf16[256,1024]{1,0:T(8,128)(2,1)}, u32[]{:S(2)}) copy-start(bf16[256,1024]{1,0:T(8,128)(2,1)} %param.17) | copy-start | bytes 1572868
  0.0 14.3 %copy-start.6 = (f32[256,8]{0,1:T(8,128)S(1)}, f32[256,8]{0,1:T(8,128)}, u32[]{:S(2)}) copy-start(f32[256,8]{0,1:T(8,128)} %param.19) | copy-start | bytes 24580
  0.0 15.6 %copy-start.8 = (f32[128,10]{0,1:T(8,128)S(1)}, f32[128,10]{0,1:T(8,128)}, u32[]{:S(2)}) copy-start(f32[128,10]{0,1:T(8,128)} %param.29) | copy-start | bytes 15364
  0.0 15.6 %copy-start.9 = (s32[128,10]{0,1:T(8,128)S(1)}, s32[128,10]{0,1:T(8,128)}, u32[]{:S(2)}) copy-start(s32[128,10]{0,1:T(8,128)} %param.28) | copy-start | bytes 15364
  1.6 14.7 %collective-permute-start = (bf16[16,2048]{1,0:T(8,128)(2,1)S(1)}, bf16[16,2048]{1,0:T(8,128)(2,1)S(1)}, u32[]{:S(2)}, u32[]{:S(2)}) collective-permute-start(bf16[16,2048]{1,0:T(8,128)(2,1)S(1)} %pad_maximum_fusion.2), channel_id=1, source_target_pairs={{0,2},{2,4},{4,6},{6,8},{8,10},{10,12},{12,14},{14,16},{16,18},{18... | collective-permute-start | bytes 196616 | tf_op jit(solution)/shard_map/ppermute | solution.py:233
  6.5 89.2 %collective-permute-start.2 = (bf16[1,2048,1024]{2,1,0:T(8,128)(2,1)}, bf16[1,2048,1024]{2,1,0:T(8,128)(2,1)}, u32[]{:S(2)}, u32[]{:S(2)}) collective-permute-start(bf16[1,2048,1024]{2,1,0:T(8,128)(2,1)} %up_mine.1), channel_id=1, source_target_pairs={{0,1},{1,0},{2,3},{3,2},{4,5},{5,4},{6,7},{7,6},{8,9},{9,8},{10,11... | collective-permute-start | bytes 12582920 | tf_op jit(solution)/shard_map/ppermute | solution.py:568
  9.0 8.4 %copy-start.5 = (s32[256]{0:T(256)}, s32[256]{0:T(256)S(1)}, u32[]{:S(2)}) copy-start(s32[256]{0:T(256)S(1)} %get-tuple-element.15) | copy-start | bytes 3076
  36.1 36.8 %copy-start = (bf16[1,512,2048]{2,1,0:T(8,128)(2,1)S(1)}, bf16[1,512,2048]{2,1,0:T(8,128)(2,1)}, u32[]{:S(2)}) copy-start(bf16[1,512,2048]{2,1,0:T(8,128)(2,1)} %down_mine.1) | copy-start | bytes 6291460
  69.1 12.6 %all-to-all-start.1 = ((bf16[16,64,128]{2,1,0:T(8,128)(2,1)}), bf16[16,64,128]{2,1,0:T(8,128)(2,1)S(1)}, u32[]{:S(2)}, u32[]{:S(2)}) async-start(bf16[16,64,128]{2,1,0:T(8,128)(2,1)} %carried_states.1), calls=%async_computation.1 | async-start | bytes 524288 | tf_op jit(solution)/shard_map/all_to_all | solution.py:254
  72.9 22.8 %collective-permute-start.3 = (bf16[1,512,2048]{2,1,0:T(8,128)(2,1)S(1)}, bf16[1,512,2048]{2,1,0:T(8,128)(2,1)}, u32[]{:S(2)}, u32[]{:S(2)}) collective-permute-start(bf16[1,512,2048]{2,1,0:T(8,128)(2,1)S(1)} %copy-done), channel_id=1, source_target_pairs={{0,1},{1,0},{2,3},{3,2},{4,5},{5,4},{6,7},{7,6},{8,9},{9,8},{10,11... | collective-permute-start | bytes 6291464 | tf_op jit(solution)/shard_map/ppermute | solution.py:569
  81.8 0.7 copy-start.1
  82.5 10.6 %copy-start.3 = (bf16[128,2048]{1,0:T(8,128)(2,1)S(1)}, bf16[128,2048]{1,0:T(8,128)(2,1)}, u32[]{:S(2)}) copy-start(bf16[128,2048]{1,0:T(8,128)(2,1)} %param.26) | copy-start | bytes 1572868
  88.6 6.1 %copy-start.7 = (f32[2048]{0:T(1024)S(1)}, f32[2048]{0:T(1024)}, u32[]{:S(2)}) copy-start(f32[2048]{0:T(1024)} %param.27) | copy-start | bytes 24580
  90.7 2.4 collective-permute-start.1
  92.3 3.4 %copy-start.4 = (f32[4,2,512]{2,1,0:T(2,128)}, f32[4,2,512]{2,1,0:T(2,128)S(1)}, u32[]{:S(2)}) copy-start(f32[4,2,512]{2,1,0:T(2,128)S(1)} %reshape.89.weight_ref) | copy-start | bytes 49156
